TPU v7x, 512 devices: a whole 4x8x8 slice. The times are simulated.
512 devices in a mesh: pipe: 2 (over y_lo), ctx: 64 (over z, x, core), tp: 4 (over y_hi).
Axes of the slice: x: 4, y: 8 (y_hi: 4, y_lo: 2; y = y_hi * 2 + y_lo), z: 8, core: 2. Of those that a mesh axis runs over, the one named last changes fastest.
Arguments:
- queries: bfloat16 [2, 8192, 2048], P('pipe', 'ctx', 'tp'), may hold values from -96 to 96
- keys: bfloat16 [2, 8192, 128], P('pipe', 'ctx'), may hold values from -4 to 4
- values: bfloat16 [2, 8192, 128], P('pipe', 'ctx'), may hold values from -6 to 6
- grad_out: bfloat16 [2, 8192, 2048], P('pipe', 'ctx', 'tp'), may hold values from -6 to 6
- span_order: int32 [2, 64, 2], P('pipe'), may hold values from 0 to 127, as said below
Outputs:
- grad_queries: bfloat16 [2, 8192, 2048], P('pipe', 'ctx', 'tp')
- grad_keys: bfloat16 [2, 8192, 128], P('pipe', 'ctx')
- grad_values: bfloat16 [2, 8192, 128], P('pipe', 'ctx')
Inputs may be any that keep to these rules, and one draw needn't show every extreme that they name: For each micro-batch m and index r, span_order[m, r, 0] is below 64 and span_order[m, r, 1] = 127 - span_order[m, r, 0]; every block number 0 to 127 appears exactly once in a micro-batch.
All inputs are finite; a program needn't handle non-finite values.
Results may differ from a plain program's by a relative error of at most 0.024.
Values may be sent and summed in bfloat16 or wider, within the bound.
A program may use at most 64 MiB of HBM per device.

v0:
```python
import jax
import jax.numpy as jnp
from jax import lax
from jax.sharding import PartitionSpec as P

very_low = -1e30


def passed_along(value, axis, steps):
    count = lax.axis_size(axis)
    pairs = [(source, (source + steps) % count) for source in range(count)]
    return lax.ppermute(value, axis, pairs)


def key_blocks(rows, positions):
    row_total = rows.shape[0]
    block_len = 512
    return (
        rows.reshape(row_total // block_len, block_len, rows.shape[1]),
        positions.reshape(row_total // block_len, block_len),
    )


def masked_scores(query_rows, query_pos, key_rows, key_pos, inv_root):
    scores = jnp.dot(query_rows, key_rows.T, preferred_element_type=jnp.float32) * inv_root
    return jnp.where(key_pos[None, :] <= query_pos[:, None], scores, -jnp.inf)


def row_stats(query_rows, query_pos, blocks, inv_root, head_dim):

    def row_advance(carried, block_pair):
        running_max, running_sum = carried
        kv_block, pos_block = block_pair
        scores = masked_scores(query_rows, query_pos, kv_block[:, :head_dim], pos_block, inv_root)
        new_max = jnp.maximum(running_max, jnp.max(scores, axis=1))
        running_sum = running_sum * jnp.exp(running_max - new_max) + jnp.sum(
            jnp.exp(scores - new_max[:, None]), axis=1
        )
        return ((new_max, running_sum), None)

    row_count = query_rows.shape[0]
    initial = (jnp.full((row_count,), very_low, jnp.float32), jnp.zeros((row_count,), jnp.float32))
    return lax.scan(row_advance, initial, blocks)[0]


def weighted_values(query_rows, query_pos, lse, blocks, inv_root, head_dim):

    def weighted_advance(accum, block_pair):
        kv_block, pos_block = block_pair
        scores = masked_scores(query_rows, query_pos, kv_block[:, :head_dim], pos_block, inv_root)
        weights = jnp.exp(scores - lse[:, None]).astype(jnp.bfloat16)
        return (
            accum + jnp.dot(weights, kv_block[:, head_dim:], preferred_element_type=jnp.float32),
            None,
        )

    initial = jnp.zeros((query_rows.shape[0], head_dim), jnp.float32)
    return lax.scan(weighted_advance, initial, blocks)[0]


def backward_pass(query_rows, query_pos, grad_rows, lse, delta, blocks, inv_root, head_dim):

    def backward_advance(accum, block_pair):
        kv_block, pos_block = block_pair
        key_part = kv_block[:, :head_dim]
        value_part = kv_block[:, head_dim:]
        scores = masked_scores(query_rows, query_pos, key_part, pos_block, inv_root)
        probs = jnp.exp(scores - lse[:, None])
        probs_low = probs.astype(jnp.bfloat16)
        grad_probs = jnp.dot(grad_rows, value_part.T, preferred_element_type=jnp.float32)
        grad_scores = (probs * (grad_probs - delta[:, None])).astype(jnp.bfloat16)
        grad_value = jnp.dot(probs_low.T, grad_rows, preferred_element_type=jnp.float32)
        grad_key = jnp.dot(grad_scores.T, query_rows, preferred_element_type=jnp.float32) * inv_root
        accum = accum + jnp.dot(grad_scores, key_part, preferred_element_type=jnp.float32)
        return (accum, jnp.concatenate([grad_key, grad_value], axis=1))

    initial = jnp.zeros((query_rows.shape[0], head_dim), jnp.float32)
    query_accum, key_grads = lax.scan(backward_advance, initial, blocks)
    return (query_accum, key_grads.reshape(-1, 2 * head_dim))


def fold_sources(received):
    return jnp.sum(received, axis=0)


def per_device(queries, keys, values, grad_out, span_order):
    tok_count = queries.shape[1]
    head_dim = keys.shape[2]
    heads_here = queries.shape[2] // head_dim
    half_len = tok_count // 2
    rank_count = lax.axis_size("ctx")
    inv_root = head_dim ** (-0.5)
    block_order = span_order[0]
    my_spans = lax.dynamic_slice_in_dim(block_order, lax.axis_index("ctx"), 1, 0)[0]
    offsets = jnp.arange(half_len, dtype=jnp.int32)
    token_pos = (my_spans[:, None] * half_len + offsets[None, :]).reshape(tok_count)
    row_count = tok_count * heads_here
    query_pos = jnp.repeat(token_pos, heads_here, total_repeat_length=row_count)
    query_rows = queries[0].reshape(row_count, head_dim)
    grad_rows = grad_out[0].reshape(row_count, head_dim)
    local_kv = jnp.concatenate([keys[0], values[0]], axis=1)
    all_kv = lax.all_gather(local_kv, "ctx", axis=0, tiled=True)
    kv_grid = all_kv.reshape(rank_count, 2, half_len, 2 * head_dim)
    pos_grid = block_order[:, :, None] * half_len + offsets[None, None, :]
    early_blocks = key_blocks(
        kv_grid[:, 0].reshape(rank_count * half_len, 2 * head_dim),
        pos_grid[:, 0].reshape(rank_count * half_len),
    )
    late_blocks = key_blocks(
        kv_grid[:, 1].reshape(rank_count * half_len, 2 * head_dim),
        pos_grid[:, 1].reshape(rank_count * half_len),
    )
    split_row = half_len * heads_here
    late_rows = query_rows[split_row:]
    late_pos = query_pos[split_row:]
    late_grads = grad_rows[split_row:]
    max_all, sum_all = row_stats(query_rows, query_pos, early_blocks, inv_root, head_dim)
    max_late, sum_late = row_stats(late_rows, late_pos, late_blocks, inv_root, head_dim)
    max_late_all = jnp.concatenate([jnp.full((split_row,), very_low, jnp.float32), max_late])
    sum_late_all = jnp.concatenate([jnp.zeros((split_row,), jnp.float32), sum_late])
    joint_max = jnp.maximum(max_all, max_late_all)
    lse = joint_max + jnp.log(
        sum_all * jnp.exp(max_all - joint_max) + sum_late_all * jnp.exp(max_late_all - joint_max)
    )
    lse_late = lse[split_row:]
    out_all = weighted_values(query_rows, query_pos, lse, early_blocks, inv_root, head_dim)
    out_late = weighted_values(late_rows, late_pos, lse_late, late_blocks, inv_root, head_dim)
    zero_rows = jnp.zeros((split_row, head_dim), jnp.float32)
    attn_out = (out_all + jnp.concatenate([zero_rows, out_late], axis=0)).astype(jnp.bfloat16)
    delta = jnp.sum(grad_rows.astype(jnp.float32) * attn_out.astype(jnp.float32), axis=1)
    query_all, early_grads = backward_pass(
        query_rows, query_pos, grad_rows, lse, delta, early_blocks, inv_root, head_dim
    )
    query_late, late_key_grads = backward_pass(
        late_rows,
        late_pos,
        late_grads,
        lse_late,
        delta[split_row:],
        late_blocks,
        inv_root,
        head_dim,
    )
    grad_query = ((query_all + jnp.concatenate([zero_rows, query_late], axis=0)) * inv_root).astype(
        jnp.bfloat16
    )
    grad_query = grad_query.reshape(1, tok_count, heads_here * head_dim)
    partial_value = jnp.stack(
        [
            early_grads.reshape(rank_count, half_len, 2 * head_dim),
            late_key_grads.reshape(rank_count, half_len, 2 * head_dim),
        ],
        axis=1,
    )
    partial_value = partial_value.reshape(rank_count, tok_count, 2 * head_dim)
    owned = fold_sources(
        lax.all_to_all(
            partial_value.astype(jnp.bfloat16), "ctx", split_axis=0, concat_axis=0, tiled=True
        ).astype(partial_value.dtype)
    )
    kv_grads = lax.psum(owned.astype(jnp.bfloat16), "tp")
    sent_query, sent_kv = passed_along((grad_query, kv_grads), "pipe", -1)
    return (sent_query, sent_kv[:, :head_dim][None], sent_kv[:, head_dim:][None])


def solution(mesh):
    return jax.shard_map(
        per_device,
        mesh=mesh,
        in_specs=(
            P("pipe", "ctx", "tp"),
            P("pipe", "ctx", None),
            P("pipe", "ctx", None),
            P("pipe", "ctx", "tp"),
            P("pipe", None, None),
        ),
        out_specs=(P("pipe", "ctx", "tp"), P("pipe", "ctx", None), P("pipe", "ctx", None)),
        check_vma=False,
    )
```

profile of v0, /device:TPU:1, one launch (start us, length us, event | category | flops | bytes accessed | tf_op | source)
XLA Modules:
  0.0 375.7 jit_solution(5835780573148097580)
XLA Ops:
  7.3 1.4 pad_maximum_fusion.1
  8.7 1.0 reshape_squeeze.6
  9.7 1.0 reshape_squeeze.7
  10.8 0.9 multiply_reduce_fusion.1
  11.8 0.8 add_add_fusion.1
  12.6 3.3 gather_fusion
  16.4 86.1 %all-gather.2.cloned.1.call-done = bf16[8192,256]{1,0:T(8,128)(2,1)} async-done(((bf16[128,256]{1,0:T(8,128)(2,1)}), bf16[8192,256]{1,0:T(8,128)(2,1)}) %all-gather.2.cloned.1.call-update) | async-done | bytes 4194320 | tf_op jit(solution)/shard_map/all_gather | solution.py:102
  102.5 4.1 %fusion.79 = (bf16[64,1,64,256]{3,2,1,0:T(8,128)(2,1)S(1)}, bf16[64,1,64,256]{3,2,1,0:T(8,128)(2,1)}) fusion(bf16[64,2,64,256]{3,2,1,0:T(8,128)(2,1)} %bitcast.212), kind=kLoop, calls=%fused_computation.132 | loop fusion | bytes 8388608 | tf_op jit(solution)/shard_map/slice | solution.py:110
  106.6 3.9 %while.76 = (s32[]{:T(128)}, f32[256]{0:T(256)S(1)}, f32[256]{0:T(256)S(1)}, s32[8,512]{1,0:T(8,128)S(1)}, s32[256]{0:T(256)S(1)}, /*index=5*/bf16[8,512,256]{2,...) while((s32[]{:T(128)}, f32[256]{0:T(256)S(1)}, f32[256]{0:T(256)S(1)}, ...), condition=%wide.region_7.8_spmd.clone, body=%wide.region_4.7_spmd.clone.sunk | while | flops 34342144 | bytes 1790072 | solution.py:43
  110.5 12.5 %while.75 = (s32[]{:T(128)}, f32[512]{0:T(512)S(1)}, f32[512]{0:T(512)S(1)}, s32[8,512]{1,0:T(8,128)S(1)}, s32[512]{0:T(512)S(1)}, /*index=5*/bf16[8,512,256]{2,...) while((s32[]{:T(128)}, f32[512]{0:T(512)S(1)}, f32[512]{0:T(512)S(1)}, ...), condition=%wide.region_3.4_spmd.clone, body=%wide.region_0.3_spmd.clone.sunk | while | flops 68684288 | bytes 2918520 | solution.py:43
  110.5 1.0 dynamic-slice_bitcast_fusion.12
  112.1 1.0 dynamic-slice_bitcast_fusion.12
  113.6 1.0 dynamic-slice_bitcast_fusion.12
  115.2 1.0 dynamic-slice_bitcast_fusion.12
  116.8 1.0 dynamic-slice_bitcast_fusion.12
  118.3 1.0 dynamic-slice_bitcast_fusion.12
  119.9 1.0 dynamic-slice_bitcast_fusion.12
  121.5 1.0 dynamic-slice_bitcast_fusion.12
  123.0 16.2 %while.78 = (s32[]{:T(128)}, f32[256,128]{1,0:T(8,128)}, s32[8,512]{1,0:T(8,128)S(1)}, s32[256]{0:T(256)S(1)}, bf16[8,512,256]{2,1,0:T(8,128)(2,1)S(1)}, /*index...) while((s32[]{:T(128)}, f32[256,128]{1,0:T(8,128)}, ...), condition=%wide.region_11.12_spmd.clone, body=%wide.region_10.11_spmd.clone.sunk | while | flops 67829760 | bytes 1122423 | solution.py:58
  123.1 1.2 fusion.152
  124.3 2.1 fusion.152
  126.5 2.1 fusion.152
  128.6 2.1 fusion.152
  130.7 2.1 fusion.152
  132.8 2.1 fusion.152
  135.0 2.1 fusion.152
  137.1 2.1 fusion.152
  139.2 13.9 %while.77 = (s32[]{:T(128)}, f32[512,128]{1,0:T(8,128)S(1)}, s32[8,512]{1,0:T(8,128)S(1)}, s32[512]{0:T(512)S(1)}, bf16[8,512,256]{2,1,0:T(8,128)(2,1)}, /*index...) while((s32[]{:T(128)}, f32[512,128]{1,0:T(8,128)S(1)}, ...), condition=%wide.region_9.10_spmd.clone, body=%wide.region_8.9_spmd.clone.sunk | while | flops 135659520 | bytes 1452151 | solution.py:58
  139.2 1.0 dynamic-slice_bitcast_fusion.14
  140.9 1.0 dynamic-slice_bitcast_fusion.14
  142.7 1.0 dynamic-slice_bitcast_fusion.14
  144.4 1.0 dynamic-slice_bitcast_fusion.14
  146.2 1.0 dynamic-slice_bitcast_fusion.14
  147.2 0.7 fusion.148
  147.9 1.0 dynamic-slice_bitcast_fusion.14
  148.9 0.7 fusion.148
  149.7 1.0 dynamic-slice_bitcast_fusion.14
  150.7 0.7 fusion.148
  151.4 1.0 dynamic-slice_bitcast_fusion.14
  152.4 0.7 fusion.148
  153.1 1.1 multiply_reduce_fusion
  154.2 1.4 broadcast.170.clone2
  155.7 28.6 %while.79 = (s32[]{:T(128)}, f32[512,128]{1,0:T(8,128)S(1)}, bf16[8,512,256]{2,1,0:T(8,128)(2,1)}, s32[8,512]{1,0:T(8,128)S(1)}, s32[512]{0:T(512)S(1)}, /*index...) while((s32[]{:T(128)}, f32[512,128]{1,0:T(8,128)S(1)}, ...), condition=%wide.region_14.15_spmd.clone, body=%wide.region_13.14_spmd.clone.sunk | while | flops 338427904 | bytes 8532115 | solution.py:78
  155.7 1.0 dynamic-slice_bitcast_fusion.16
  159.2 1.0 dynamic-slice_bitcast_fusion.16
  162.8 1.0 dynamic-slice_bitcast_fusion.16
  166.4 1.0 dynamic-slice_bitcast_fusion.16
  169.2 0.7 constant_dynamic-update-slice_fusion.4
  170.0 1.0 dynamic-slice_bitcast_fusion.16
  173.5 1.0 dynamic-slice_bitcast_fusion.16
  177.1 1.0 dynamic-slice_bitcast_fusion.16
  180.7 1.0 dynamic-slice_bitcast_fusion.16
  184.2 1.5 broadcast.170.clone2.1
  185.7 17.6 %while.80 = (s32[]{:T(128)}, f32[256,128]{1,0:T(8,128)S(1)}, bf16[8,512,256]{2,1,0:T(8,128)(2,1)}, s32[8,512]{1,0:T(8,128)S(1)}, s32[256]{0:T(256)S(1)}, /*index...) while((s32[]{:T(128)}, f32[256,128]{1,0:T(8,128)S(1)}, ...), condition=%wide.region_16.17_spmd.clone, body=%wide.region_15.16_spmd.clone.sunk | while | flops 169541632 | bytes 5645459 | solution.py:78
  198.2 0.7 constant_dynamic-update-slice_fusion.5
  203.3 2.6 pad_maximum_fusion
  205.9 2.3 copy.18
  208.2 6.4 %all-to-all-start = ((bf16[64,128,256]{2,1,0:T(8,128)(2,1)}), bf16[64,128,256]{2,1,0:T(8,128)(2,1)}, u32[]{:S(2)}, u32[]{:S(2)}) async-start(bf16[64,128,256]{2,1,0:T(8,128)(2,1)} %bitcast.209), calls=%async_computation | async-start | bytes 8388608 | tf_op jit(solution)/shard_map/all_to_all | solution.py:157
  214.8 3.1 collective-permute-start
  217.9 91.1 %all-to-all-done = bf16[64,128,256]{2,1,0:T(8,128)(2,1)} async-done(((bf16[64,128,256]{2,1,0:T(8,128)(2,1)}), bf16[64,128,256]{2,1,0:T(8,128)(2,1)}, u32[]{:S(2)}, u32[]{:S(2)}) %all-to-all-start) | async-done | bytes 4194336 | tf_op jit(solution)/shard_map/all_to_all | solution.py:157
  309.0 3.4 reduce_sum.40
  312.4 50.0 %all-reduce.6.cloned.1.call-done = bf16[128,256]{1,0:T(8,128)(2,1)} async-done(((bf16[128,256]{1,0:T(8,128)(2,1)}), bf16[128,256]{1,0:T(8,128)(2,1)}) %all-reduce.6.cloned.1.call-update) | async-done | bytes 65552 | tf_op jit(solution)/shard_map/psum | solution.py:161
  362.4 2.8 collective-permute-start.1
  365.2 2.4 collective-permute-done.1
  (324 shorter events, 49.4 us)
Async XLA Ops:
  7.2 8.8 %copy-start = (s32[4,128]{1,0:T(4,128)S(1)}, s32[4,128]{1,0:T(4,128)}, u32[]{:S(2)}) copy-start(s32[4,128]{1,0:T(4,128)} %constant.180.clone.1) | copy-start | bytes 6148
  7.2 9.1 %slice-start = ((bf16[1,128,512]{2,1,0:T(8,128)(2,1)}), bf16[1,64,512]{2,1,0:T(8,128)(2,1)S(1)}, s32[]{:S(2)}) async-start(bf16[1,128,512]{2,1,0:T(8,128)(2,1)} %param.19), calls=%async_computation.3 | async-start | bytes 131072 | tf_op jit(solution)/shard_map/slice | solution.py:114
  7.2 9.1 %slice-start.1 = ((bf16[1,128,512]{2,1,0:T(8,128)(2,1)}), bf16[1,64,512]{2,1,0:T(8,128)(2,1)S(1)}, s32[]{:S(2)}) async-start(bf16[1,128,512]{2,1,0:T(8,128)(2,1)} %param.22), calls=%async_computation.4 | async-start | bytes 131072 | tf_op jit(solution)/shard_map/slice | solution.py:116
  7.2 8.8 %copy-start.1 = (s32[1,64,2]{1,2,0:T(2,128)S(1)}, s32[1,64,2]{1,2,0:T(2,128)}, u32[]{:S(2)}) copy-start(s32[1,64,2]{1,2,0:T(2,128)} %param.23) | copy-start | bytes 1540
  7.2 95.2 %all-gather.2.cloned.1.call-start = ((), (), s32[]{:S(2)}) async-start(), calls=%async_computation.1 | async-start | bytes 4259840 | tf_op jit(solution)/shard_map/all_gather | solution.py:102
  208.2 100.8 %all-to-all-start = ((bf16[64,128,256]{2,1,0:T(8,128)(2,1)}), bf16[64,128,256]{2,1,0:T(8,128)(2,1)}, u32[]{:S(2)}, u32[]{:S(2)}) async-start(bf16[64,128,256]{2,1,0:T(8,128)(2,1)} %bitcast.209), calls=%async_computation | async-start | bytes 8388608 | tf_op jit(solution)/shard_map/all_to_all | solution.py:157
  214.6 147.8 %all-reduce.6.cloned.1.call-start = ((), (), s32[]{:S(2)}) async-start(), calls=%async_computation.2 | async-start | bytes 131072 | tf_op jit(solution)/shard_map/psum | solution.py:161
  214.8 150.5 %collective-permute-start = (bf16[1,128,512]{2,1,0:T(8,128)(2,1)S(1)}, bf16[1,128,512]{2,1,0:T(8,128)(2,1)S(1)}, u32[]{:S(2)}, u32[]{:S(2)}) collective-permute-start(bf16[1,128,512]{2,1,0:T(8,128)(2,1)S(1)} %reshape.135), channel_id=1, source_target_pairs={{0,256},{256,0},{1,257},{257,1},{2,258},{258,2},{3,259},{259,3},{4... | collective-permute-start | bytes 393224 | tf_op jit(solution)/shard_map/ppermute | solution.py:12
  362.4 5.2 %collective-permute-start.1 = (bf16[128,256]{1,0:T(8,128)(2,1)}, bf16[128,256]{1,0:T(8,128)(2,1)S(1)}, u32[]{:S(2)}, u32[]{:S(2)}) collective-permute-start(bf16[128,256]{1,0:T(8,128)(2,1)} %all-reduce.6.cloned.1.call-done), channel_id=1, source_target_pairs={{0,256},{256,0},{1,257},{257,1},{2,258},{258,2},{3,259},{259,3},{4... | collective-permute-start | bytes 196616 | tf_op jit(solution)/shard_map/ppermute | solution.py:12
Sparse Core Ops, SparseCore 0:
  11.4 91.0 all-gather.1
  312.6 49.8 all-reduce.5
where the time goes:
time: 379 us; the launch traced here: 376 us
  waiting for transfers between devices  230 us (61%)
  local copies, waits for them, and re-layouts  54.3 us (14%)
  matrix products  49.7 us (13%)
  between operations  14.3 us (4%)
  other arithmetic  13.7 us (4%)
  starting transfers between devices  12.4 us (3%)
    all_to_all x1, waiting for transfers between devices, per_device(): lax.all_to_all(partial_value.astype(jnp.bfloat16), 'ctx', split_axis=0, c...  91.1 us
    all_gather x1, waiting for transfers between devices, per_device(): all_kv = lax.all_gather(local_kv, 'ctx', axis=0, tiled=True)  86.1 us
    psum x1, waiting for transfers between devices, per_device(): kv_grads = lax.psum(owned.astype(jnp.bfloat16), 'tp')  50 us
    squeeze x48, local copies, waits for them, and re-layouts, row_stats(): return lax.scan(row_advance, initial, blocks)[0]  23.8 us
    dot_general x16, matrix products, weighted_advance(): jnp.dot(weights, kv_block[:, head_dim:], preferred_element_type=jnp.float32)  21.7 us
    dynamic_update_slice x32, local copies, waits for them, and re-layouts, backward_pass(): query_accum, key_grads = lax.scan(backward_advance, initial, blocks)  13.7 us
    dot_general x32, matrix products, masked_scores(): jnp.dot(query_rows, key_rows.T, preferred_element_type=jnp.float32)  9.84 us
  transfers between devices with their start and end apart: 5, of which 4 were waited for; matrix products, arithmetic and copies ran while one was open for 3% of the time, Pallas kernels for 0%

commit v1 on v0

v1 whole, which is shorter than its diff:
```python
import functools

import jax
import jax.numpy as jnp
from jax import lax
from jax.experimental import pallas as pl
from jax.experimental.pallas import tpu as pltpu
from jax.sharding import PartitionSpec as P

MESH = pl.DeviceIdType.MESH
F32 = jnp.float32
BF16 = jnp.bfloat16

NZ = 8
NX = 4
NT = 4
HEADS = 4
HALF = 64
HD = 128
ROW = 2 * NX
ROWS = HEADS * HALF
KEYS = ROW * HALF
INV_ROOT = HD ** (-0.5)
LOG2E = 1.4426950408889634
NEG = -1e30
POS = 1e30


def dot_nt(a, b):
    return lax.dot_general(a, b, (((1,), (1,)), ((), ())), preferred_element_type=F32)


def dot_nn(a, b):
    return jnp.dot(a, b, preferred_element_type=F32)


def dot_tn(a, b):
    return lax.dot_general(a, b, (((0,), (0,)), ((), ())), preferred_element_type=F32)


def col_sum(v):
    return jnp.sum(v, axis=0, keepdims=True)


def col_max(v):
    return jnp.max(v, axis=0, keepdims=True)


def kernel(
    q_ref, k_ref, v_ref, g_ref, span_ref,
    dq_out, dk_out, dv_out,
    kbuf, vbuf, s1, s2, dp1, dp2, kselbuf, qq, oo, dql, dq2, dqst,
    pk, pv, sib, rr, cr, xr, zr, ysum, yr,
    p1send, p1k, p1v, fsend, frecv, csend, crecv, d2d_send, d2d_recv,
    sib_send, sib_recv, rsend, rrecv, bsend, brecv, xsend, xrecv, zsend, zrecv,
    ysend, yrecv, dqsem,
):
    pipe = lax.axis_index("pipe")
    me = lax.axis_index("ctx")
    t = lax.axis_index("tp")
    z = me // (2 * NX)
    x = (me // 2) % NX
    c = me % 2
    y = t * 2 + pipe

    def at(zz, xx, cc):
        return (pipe, (zz * NX + xx) * 2 + cc, t)

    def zoff(d):
        return lax.rem(z + d + NZ, NZ)

    def xoff(d):
        return lax.rem(x + d + NX, NX)

    def other(tt, cc):
        return (1 - pipe, (z * NX + x) * 2 + cc, tt)

    sibling = at(z, x, 1 - c)

    def remote(src, dst, ssem, rsem, dev):
        return pltpu.make_async_remote_copy(
            src_ref=src, dst_ref=dst, send_sem=ssem, recv_sem=rsem,
            device_id=dev, device_id_type=MESH,
        )

    barrier = pltpu.get_barrier_semaphore()
    count = 0

    def greet(dev):
        pl.semaphore_signal(barrier, inc=1, device_id=dev, device_id_type=MESH)

    greet(sibling)
    count += 1
    for cc in range(2):
        for d in range(1, NX):
            greet(at(z, xoff(d), cc))
            count += 1
        for d in range(1, NZ):
            greet(at(zoff(d), x, cc))
            count += 1
        for tt in range(NT):
            greet(other(tt, cc))
            count += 1
    pl.semaphore_wait(barrier, count)

    def first_k(d):
        return remote(k_ref.at[0], kbuf.at[me], p1send.at[d], p1k.at[2 * d + c], at(z, xoff(d), 0))

    def first_v(d):
        return remote(v_ref.at[0], vbuf.at[z, x, c], p1send.at[NX + d], p1v.at[2 * d + c],
                      at(zoff(d), x, 1))

    for d in range(1, NX):
        first_k(d).start()

    @pl.when(c == 1)
    def _():
        first_k(0).start()
        vbuf[z, x, 1] = v_ref[0]

    @pl.when(c == 0)
    def _():
        first_v(0).start()
        kbuf[me] = k_ref[0]

    for d in (1, 7, 2, 6, 3, 5, 4):
        first_v(d).start()

    def k_part(row, h):
        return pl.ds(row * ROW + h * (ROW // 2), ROW // 2)

    def fwd_k(way, k, h):
        step = 1 if way == 0 else -1
        part = k_part(zoff(-step * (k - 1)), h)
        i = (way * 4 + k - 1) * 2 + h
        return remote(kbuf.at[part], kbuf.at[part], fsend.at[i], frecv.at[i], at(zoff(step), x, 0))

    def got_k(way, k, h):
        step = 1 if way == 0 else -1
        return k_part(zoff(-step * k), h)

    def d2d_k(part, i):
        return remote(kbuf.at[part], kbuf.at[part], d2d_send.at[i], d2d_recv.at[i], sibling)

    def fwd_v(way, k, h):
        step = 1 if way == 0 else -1
        ref = vbuf.at[pl.ds(2 * h, 2), xoff(-step * (k - 1))]
        i = (way * 2 + k - 1) * 4 + h
        return remote(ref, ref, csend.at[i], crecv.at[i], at(z, xoff(step), 1))

    def d2d_v(col, h, i):
        ref = vbuf.at[pl.ds(2 * h, 2), col]
        return remote(ref, ref, d2d_send.at[i], d2d_recv.at[i], sibling)

    k_steps = [(w, k, h) for k in range(1, 5) for h in range(2) for w in range(2)
               if k < 4 or h == w]
    v_first = [(w, 1, (h + 2 * w) % 4) for h in range(4) for w in range(2)]
    v_steps = v_first + [(w, 2, h + 2 * w) for h in range(2) for w in range(2)]

    @pl.when(c == 0)
    def _():
        sent = []
        for d in range(NX):
            for cc in range(2):
                if (d, cc) != (0, 0):
                    pltpu.make_async_copy(kbuf.at[0], kbuf.at[0], p1k.at[2 * d + cc]).wait()
        for h in range(2):
            for w in range(2):
                cp = fwd_k(w, 1, h)
                cp.start()
                sent.append(cp)
        for h in range(2):
            cp = d2d_k(k_part(z, h), h)
            cp.start()
            sent.append(cp)
        for n, (w, k, h) in enumerate(k_steps):
            fwd_k(w, k, h).wait_recv()
            if k < 3 or (k == 3 and h == w):
                cp = fwd_k(w, k + 1, h)
                cp.start()
                sent.append(cp)
            cp = d2d_k(got_k(w, k, h), n + 2)
            cp.start()
            sent.append(cp)
        for cp in sent:
            cp.wait_send()
        for i in range(16):
            d2d_v(0, 0, i).wait_recv()
        first_v(0).wait_send()

    @pl.when(c == 1)
    def _():
        sent = []
        for d in range(NZ):
            for cc in range(2):
                if (d, cc) != (0, 1):
                    pltpu.make_async_copy(kbuf.at[0], kbuf.at[0], p1v.at[2 * d + cc]).wait()
        for (w, k, h) in v_first:
            cp = fwd_v(w, 1, h)
            cp.start()
            sent.append(cp)
        for h in range(4):
            cp = d2d_v(x, h, h)
            cp.start()
            sent.append(cp)
        for n, (w, k, h) in enumerate(v_steps):
            fwd_v(w, k, h).wait_recv()
            if k == 1 and h // 2 == w:
                cp = fwd_v(w, 2, h)
                cp.start()
                sent.append(cp)
            step = 1 if w == 0 else -1
            cp = d2d_v(xoff(-step * k), h, n + 4)
            cp.start()
            sent.append(cp)
        for cp in sent:
            cp.wait_send()
        for i in range(16):
            d2d_k(k_part(0, 0), i).wait_recv()
        first_k(0).wait_send()

    for d in range(1, NX):
        first_k(d).wait_send()
    for d in range(1, NZ):
        first_v(d).wait_send()

    for h in range(HEADS):
        cols = slice(h * HD, (h + 1) * HD)
        rows = slice(h * HALF, (h + 1) * HALF)
        qq[rows, 0:HD] = q_ref[0, 0:HALF, cols]
        qq[rows, HD:2 * HD] = q_ref[0, HALF:2 * HALF, cols]
        oo[rows, 0:HD] = g_ref[0, 0:HALF, cols]
        oo[rows, HD:2 * HD] = g_ref[0, HALF:2 * HALF, cols]

    my_block = span_ref[0, me, 0]

    def early(b, i):
        return span_ref[0, b * ROW + i, 0] < my_block

    def pick(buf, b):
        e, both = [], []
        for i in range(ROW):
            if buf is kbuf:
                blk = buf[b * ROW + i]
            else:
                blk = buf[b, i // 2, i % 2]
            lo, hi = blk[:HALF], blk[HALF:]
            s = early(b, i)
            zero = jnp.zeros_like(lo)
            e.append(lo)
            both.append(jnp.concatenate([jnp.where(s, lo, zero), jnp.where(s, zero, hi)], axis=1))
        return jnp.concatenate(e, axis=0), jnp.concatenate(both, axis=0)

    scale = INV_ROOT * LOG2E

    def sweep_scores(b, carry):
        m_e, m_l = carry
        ke, ksel = pick(kbuf, b)
        kselbuf[b] = ksel
        s1[b] = dot_nt(ke, qq[:, HD:]) * scale
        s2[b] = dot_nt(ksel, qq[...]) * scale
        m_l = jnp.maximum(m_l, col_max(s1[b]))
        for i in range(ROW):
            top = col_max(s2[b, i * HALF:(i + 1) * HALF])
            s = early(b, i)
            mine = b * ROW + i == me
            low = jnp.full_like(top, NEG)
            top = jnp.where(mine, low, top)
            m_e = jnp.maximum(m_e, jnp.where(s, top, low))
            m_l = jnp.maximum(m_l, jnp.where(s, low, top))
        return m_e, m_l

    start = jnp.full((1, ROWS), NEG, F32)
    m_e, m_l = lax.fori_loop(0, NZ, sweep_scores, (start, start))

    key_no = lax.broadcasted_iota(jnp.int32, (HALF, ROWS), 0)
    tok_no = lax.broadcasted_iota(jnp.int32, (HALF, ROWS), 1) % HALF
    seen = key_no <= tok_no
    k_e, k_l = k_ref[0, :HALF], k_ref[0, HALF:]
    v_e, v_l = v_ref[0, :HALF], v_ref[0, HALF:]
    q_e, q_l = qq[:, :HD], qq[:, HD:]
    o_e, o_l = oo[:, :HD], oo[:, HD:]
    see = jnp.where(seen, dot_nt(k_e, q_e) * scale, NEG)
    sll = jnp.where(seen, dot_nt(k_l, q_l) * scale, NEG)
    m_e = jnp.maximum(m_e, col_max(see))
    m_l = jnp.maximum(m_l, col_max(sll))
    pee = jnp.exp2(see - m_e)
    pll = jnp.exp2(sll - m_l)
    dpee = dot_nt(v_e, o_e)
    dpll = dot_nt(v_l, o_l)

    def sweep_sums(b, carry):
        l_e, l_l, d_e, d_l = carry
        ve, vsel = pick(vbuf, b)
        dp1[b] = dot_nt(ve, oo[:, HD:])
        dp2[b] = dot_nt(vsel, oo[...])
        for i in range(ROW):
            part = slice(i * HALF, (i + 1) * HALF)
            p = jnp.exp2(s1[b, part] - m_l)
            s1[b, part] = p
            l_l = l_l + col_sum(p)
            d_l = d_l + col_sum(p * dp1[b, part])
            s = early(b, i)
            top = jnp.where(s, m_e, m_l)
            top = jnp.where(b * ROW + i == me, jnp.full_like(top, POS), top)
            p = jnp.exp2(s2[b, part] - top)
            s2[b, part] = p
            ps = col_sum(p)
            pd = col_sum(p * dp2[b, part])
            zero = jnp.zeros_like(ps)
            l_e = l_e + jnp.where(s, ps, zero)
            l_l = l_l + jnp.where(s, zero, ps)
            d_e = d_e + jnp.where(s, pd, zero)
            d_l = d_l + jnp.where(s, zero, pd)
        return l_e, l_l, d_e, d_l

    l_e, l_l, d_e, d_l = lax.fori_loop(
        0, NZ, sweep_sums,
        (col_sum(pee), col_sum(pll), col_sum(pee * dpee), col_sum(pll * dpll)),
    )
    r_e = 1.0 / l_e
    r_l = 1.0 / l_l
    d_e = d_e * r_e
    d_l = d_l * r_l

    pee = pee * r_e
    pll = pll * r_l
    dsee = (pee * (dpee - d_e)).astype(BF16)
    dsll = (pll * (dpll - d_l)).astype(BF16)
    own_k_e = dot_nn(dsee, q_e) * INV_ROOT
    own_k_l = dot_nn(dsll, q_l) * INV_ROOT
    own_v_e = dot_nn(pee.astype(BF16), o_e)
    own_v_l = dot_nn(pll.astype(BF16), o_l)
    dq2[0:HD] = dot_tn(k_e, dsee)
    dq2[HD:2 * HD] = dot_tn(k_l, dsll)
    dql[...] = jnp.zeros_like(dql)

    def sib_send_k(b):
        part = pl.ds(b * ROW, ROW)
        return remote(pk.at[part], sib.at[part], sib_send.at[b], sib_recv.at[b], sibling)

    def sib_send_v(b):
        part = pl.ds(b * ROW, ROW)
        return remote(pv.at[part], sib.at[part], sib_send.at[b], sib_recv.at[b], sibling)

    def sweep_grads(b, _):
        ke_list = [kbuf[b * ROW + i, :HALF] for i in range(ROW)]
        ke = jnp.concatenate(ke_list, axis=0)
        ksel = kselbuf[b]
        p1 = s1[b] * r_l
        ds1 = (p1 * (dp1[b] - d_l)).astype(BF16)
        p1 = p1.astype(BF16)
        p2s, ds2s = [], []
        for i in range(ROW):
            part = slice(i * HALF, (i + 1) * HALF)
            s = early(b, i)
            p = s2[b, part] * jnp.where(s, r_e, r_l)
            ds2s.append((p * (dp2[b, part] - jnp.where(s, d_e, d_l))).astype(BF16))
            p2s.append(p.astype(BF16))
        p2 = jnp.concatenate(p2s, axis=0)
        ds2 = jnp.concatenate(ds2s, axis=0)
        v1 = dot_nn(p1, oo[:, HD:])
        v2 = dot_nn(p2, oo[...])
        k1 = dot_nn(ds1, qq[:, HD:]) * INV_ROOT
        k2 = dot_nn(ds2, qq[...]) * INV_ROOT
        dql[...] += dot_tn(ke, ds1)
        dq2[...] += dot_tn(ksel, ds2)
        for i in range(ROW):
            part = slice(i * HALF, (i + 1) * HALF)
            s = early(b, i)
            zero = jnp.zeros((HALF, HD), F32)
            pv[b * ROW + i, :HALF] = (v1[part] + jnp.where(s, v2[part, :HD], zero)).astype(BF16)
            pv[b * ROW + i, HALF:] = jnp.where(s, zero, v2[part, HD:]).astype(BF16)
            pk[b * ROW + i, :HALF] = (k1[part] + jnp.where(s, k2[part, :HD], zero)).astype(BF16)
            pk[b * ROW + i, HALF:] = jnp.where(s, zero, k2[part, HD:]).astype(BF16)

        @pl.when(b == z)
        def _():
            pv[me, :HALF] = (pv[me, :HALF].astype(F32) + own_v_e).astype(BF16)
            pv[me, HALF:] = (pv[me, HALF:].astype(F32) + own_v_l).astype(BF16)
            pk[me, :HALF] = (pk[me, :HALF].astype(F32) + own_k_e).astype(BF16)
            pk[me, HALF:] = (pk[me, HALF:].astype(F32) + own_k_l).astype(BF16)

        @pl.when(c == 0)
        def _():
            sib_send_v(b).start()

        @pl.when(c == 1)
        def _():
            sib_send_k(b).start()

        return 0

    lax.fori_loop(0, NZ, sweep_grads, 0)

    for j, acc in enumerate((dq2[0:HD], dq2[HD:2 * HD] + dql[...])):
        g = (acc * INV_ROOT).T.astype(BF16)
        for h in range(HEADS):
            dqst[j * HALF:(j + 1) * HALF, h * HD:(h + 1) * HD] = g[h * HALF:(h + 1) * HALF]
    dq_copy = remote(dqst, dq_out.at[0], dqsem.at[0], dqsem.at[1], other(t, c))
    dq_copy.start()

    def add_into(dst, idx, *terms):
        total = dst[idx].astype(F32)
        for ref, i in terms:
            total = total + ref[i].astype(F32)
        dst[idx] = total.astype(BF16)

    @pl.when(c == 0)
    def _():
        for b in range(NZ):
            sib_send_k(b).wait_recv()
        sent = []

        def slot(way, k, h):
            return (way, k - 1, pl.ds(h * (ROW // 2), ROW // 2))

        def send(way, k, h):
            step = 1 if way == 0 else -1
            i = (way * 4 + k - 1) * 2 + h
            return remote(pk.at[k_part(zoff(step * k), h)], rr.at[slot(way, k, h)],
                          rsend.at[i], rrecv.at[i], at(zoff(step), x, 0))

        def hop(way, k, h, has):
            step = 1 if way == 0 else -1
            part = k_part(zoff(step * k), h)
            terms = [(sib, part)]
            if has:
                send(way, k + 1, h).wait_recv()
                terms.append((rr, slot(way, k + 1, h)))
            add_into(pk, part, *terms)
            cp = send(way, k, h)
            cp.start()
            sent.append(cp)

        hop(0, 4, 0, False)
        hop(1, 4, 1, False)
        hop(0, 3, 1, False)
        hop(1, 3, 0, False)
        hop(0, 3, 0, True)
        hop(1, 3, 1, True)
        for k in (2, 1):
            for h in (1, 0):
                hop(0, k, h, True)
                hop(1, k, 1 - h, True)
        for h in (1, 0):
            for w, hh in ((0, h), (1, 1 - h)):
                send(w, 1, hh).wait_recv()
        for h in range(2):
            add_into(pk, k_part(z, h), (sib, k_part(z, h)), (rr, slot(0, 1, h)), (rr, slot(1, 1, h)))

        def across(d):
            return remote(pk.at[pl.ds(z * ROW + 2 * xoff(d), 2)], xr.at[d], xsend.at[d],
                          xrecv.at[d], at(z, xoff(d), 0))

        for d in range(1, NX):
            across(d).start()
        for d in range(1, NX):
            across(d).wait_recv()
        mine = pl.ds(z * ROW + 2 * x, 2)
        total = pk[mine].astype(F32)
        for d in range(1, NX):
            total = total + xr[d].astype(F32)
        ysum[...] = total.astype(BF16)
        for d in range(1, NX):
            across(d).wait_send()
        for cp in sent:
            cp.wait_send()
        for b in range(NZ):
            sib_send_v(b).wait_send()

    @pl.when(c == 1)
    def _():
        for b in range(NZ):
            sib_send_v(b).wait_recv()
        sent = []

        def cell(zz, xx):
            return pl.ds((zz * NX + xx) * 2, 2)

        def send(way, k, h, j):
            step = 1 if way == 0 else -1
            zz = 2 * h + j
            i = (way * 2 + k - 1) * NZ + zz
            return remote(pv.at[cell(zz, xoff(step * k))], cr.at[way, k - 1, zz],
                          bsend.at[i], brecv.at[i], at(z, xoff(step), 1))

        def hop(way, k, h, has):
            step = 1 if way == 0 else -1
            for j in range(2):
                zz = 2 * h + j
                part = cell(zz, xoff(step * k))
                terms = [(sib, part)]
                if has:
                    send(way, k + 1, h, j).wait_recv()
                    terms.append((cr, (way, k, zz)))
                add_into(pv, part, *terms)
                cp = send(way, k, h, j)
                cp.start()
                sent.append(cp)

        for h in range(2):
            hop(0, 2, h, False)
            hop(1, 2, h + 2, False)
        for h in range(2):
            hop(0, 1, h + 2, False)
            hop(1, 1, h, False)
        for h in range(2):
            hop(0, 1, h, True)
            hop(1, 1, h + 2, True)

        def across(d):
            return remote(pv.at[cell(zoff(d), x)], zr.at[d], zsend.at[d], zrecv.at[d],
                          at(zoff(d), x, 1))

        for zz in range(NZ):
            for w in range(2):
                send(w, 1, zz // 2, zz % 2).wait_recv()
            add_into(pv, cell(zz, x), (sib, cell(zz, x)), (cr, (0, 0, zz)), (cr, (1, 0, zz)))
        for d in (4, 3, 5, 2, 6, 1, 7):
            across(d).start()
        for d in range(1, NZ):
            across(d).wait_recv()
        total = pv[cell(z, x)].astype(F32)
        for d in range(1, NZ):
            total = total + zr[d].astype(F32)
        ysum[...] = total.astype(BF16)
        for d in range(1, NZ):
            across(d).wait_send()
        for cp in sent:
            cp.wait_send()
        for b in range(NZ):
            sib_send_k(b).wait_send()

    def last(tt, cc):
        i = tt * 2 + cc
        return remote(ysum.at[cc], yr.at[c, t], ysend.at[i], yrecv.at[c, t], other(tt, cc))

    for tt in range(NT):
        for cc in range(2):
            last(tt, cc).start()
    for kind in range(2):
        for tt in range(NT):
            pltpu.make_async_copy(ysum.at[0], ysum.at[0], yrecv.at[kind, tt]).wait()
    for kind, out in ((0, dk_out), (1, dv_out)):
        total = yr[kind, 0].astype(F32)
        for tt in range(1, NT):
            total = total + yr[kind, tt].astype(F32)
        out[0] = total.astype(BF16)
    for tt in range(NT):
        for cc in range(2):
            last(tt, cc).wait_send()
    dq_copy.wait()


def per_device(queries, keys, values, grad_out, span_order):
    vmem = pl.BlockSpec(memory_space=pltpu.VMEM)
    dma = pltpu.SemaphoreType.DMA
    scratch = [
        pltpu.VMEM((NZ * ROW, 128, HD), BF16),
        pltpu.VMEM((NZ, NX, 2, 128, HD), BF16),
        pltpu.VMEM((NZ, KEYS, ROWS), F32),
        pltpu.VMEM((NZ, KEYS, ROWS), F32),
        pltpu.VMEM((NZ, KEYS, ROWS), F32),
        pltpu.VMEM((NZ, KEYS, ROWS), F32),
        pltpu.VMEM((NZ, KEYS, 2 * HD), BF16),
        pltpu.VMEM((ROWS, 2 * HD), BF16),
        pltpu.VMEM((ROWS, 2 * HD), BF16),
        pltpu.VMEM((HD, ROWS), F32),
        pltpu.VMEM((2 * HD, ROWS), F32),
        pltpu.VMEM((128, HEADS * HD), BF16),
        pltpu.VMEM((NZ * ROW, 128, HD), BF16),
        pltpu.VMEM((NZ * ROW, 128, HD), BF16),
        pltpu.VMEM((NZ * ROW, 128, HD), BF16),
        pltpu.VMEM((2, 4, ROW, 128, HD), BF16),
        pltpu.VMEM((2, 2, NZ, 2, 128, HD), BF16),
        pltpu.VMEM((NX, 2, 128, HD), BF16),
        pltpu.VMEM((NZ, 2, 128, HD), BF16),
        pltpu.VMEM((2, 128, HD), BF16),
        pltpu.VMEM((2, NT, 128, HD), BF16),
        dma((NX + NZ,)), dma((2 * NX,)), dma((2 * NZ,)),
        dma((16,)), dma((16,)), dma((16,)), dma((16,)),
        dma((16,)), dma((16,)),
        dma((NZ,)), dma((NZ,)),
        dma((16,)), dma((16,)), dma((32,)), dma((32,)),
        dma((NX,)), dma((NX,)), dma((NZ,)), dma((NZ,)),
        dma((8,)), dma((2, NT)), dma((2,)),
    ]
    return pl.pallas_call(
        kernel,
        out_shape=(
            jax.ShapeDtypeStruct(queries.shape, BF16),
            jax.ShapeDtypeStruct(keys.shape, BF16),
            jax.ShapeDtypeStruct(values.shape, BF16),
        ),
        in_specs=[vmem, vmem, vmem, vmem, pl.BlockSpec(memory_space=pltpu.SMEM)],
        out_specs=(pl.BlockSpec(memory_space=pl.ANY), vmem, vmem),
        scratch_shapes=scratch,
        compiler_params=pltpu.CompilerParams(
            collective_id=1, has_side_effects=True, vmem_limit_bytes=56 * 2**20
        ),
        name="attention_backward",
    )(queries, keys, values, grad_out, span_order)


def solution(mesh):
    return jax.shard_map(
        per_device,
        mesh=mesh,
        in_specs=(
            P("pipe", "ctx", "tp"),
            P("pipe", "ctx", None),
            P("pipe", "ctx", None),
            P("pipe", "ctx", "tp"),
            P("pipe", None, None),
        ),
        out_specs=(P("pipe", "ctx", "tp"), P("pipe", "ctx", None), P("pipe", "ctx", None)),
        check_vma=False,
    )
```

time: 379 us -> 93 us (0.25)
  waiting for transfers between devices: 230 us -> 0 us
  Pallas kernels: 0 us -> 87.7 us
  local copies, waits for them, and re-layouts: 54.3 us -> 4.34 us
  matrix products: 49.7 us -> 0 us
  other arithmetic: 13.7 us -> 0 us
  between operations: 14.3 us -> 0.65 us
  starting transfers between devices: 12.4 us -> 0 us
    all_to_all x1 -> x0, waiting for transfers between devices: 91.1 us -> none  [per_device(): lax.all_to_all(partial_value.astype(jnp.bfloat16), 'ctx', split_axis=0, c...]
    pallas_call x0 -> x1, Pallas kernels: none -> 87.7 us  [per_device(): pl.pallas_call(kernel, out_shape=(jax.ShapeDtypeStruct(queries.shape, BF1...]
    all_gather x1 -> x0, waiting for transfers between devices: 86.1 us -> none  [per_device(): all_kv = lax.all_gather(local_kv, 'ctx', axis=0, tiled=True)]
    psum x1 -> x0, waiting for transfers between devices: 50 us -> none  [per_device(): kv_grads = lax.psum(owned.astype(jnp.bfloat16), 'tp')]
    dot_general x112 -> x0, matrix products: 49.7 us -> none  [the longest x16 21.7 us: weighted_advance(): jnp.dot(weights, kv_block[:, head_dim:], preferred_element_type=jnp.float32)]
    squeeze x48 -> x0, local copies, waits for them, and re-layouts: 23.8 us -> none  [row_stats(): return lax.scan(row_advance, initial, blocks)[0]]
    dynamic_update_slice x32 -> x0, local copies, waits for them, and re-layouts: 13.7 us -> none  [backward_pass(): query_accum, key_grads = lax.scan(backward_advance, initial, blocks)]
    another operation x7 -> x0, local copies, waits for them, and re-layouts: 7.32 us -> none
  transfers between devices with their start and end apart: 5 -> 0, of which waited for: 4 -> 0; matrix products, arithmetic and copies ran while one was open for 3% -> 0% of each run, Pallas kernels for 0% -> 0%
where the time goes in v1:
time: 93 us; the launch traced here: 92.7 us
  Pallas kernels  87.7 us (94%)
  local copies, waits for them, and re-layouts  4.34 us (5%)
    pallas_call x1, Pallas kernels, per_device(): pl.pallas_call(kernel, out_shape=(jax.ShapeDtypeStruct(queries.shape, BF1...  87.7 us
    unnamed x8, local copies, waits for them, and re-layouts  4.34 us

profile of v1, /device:TPU:1, one launch (start us, length us, event | category | flops | bytes accessed | tf_op | source)
XLA Modules:
  0.0 92.7 jit_solution(11456220945794205285)
XLA Ops:
  0.6 1.4 %copy.8.span_ref = s32[1,64,2]{2,1,0:T(8,128)} copy(s32[1,64,2]{1,2,0:T(2,128)} %param.9) | data formatting | bytes 1024 | tf_op args[4]
  2.0 87.7 %attention_backward.1 = (bf16[1,128,512]{2,1,0:T(8,128)(2,1)}, bf16[1,128,128]{2,1,0:T(8,128)(2,1)}, bf16[1,128,128]{2,1,0:T(8,128)(2,1)}) custom-call(bf16[1,128,512]{2,1,0:T(8,128)(2,1)} %q_ref.1, bf16[1,128,128]{2,1,0:T(8,128)(2,1)} %k_ref.1, bf16[1,128,128]{2,1,0:T(8,128)(2,1)} %v_ref.1, bf16[1,128,512]{2,1,0:T(8,128)(2,1)} %g_ref.1, ...), custom_call_target="tpu_custom_call" | custom-call | tf_op jit(solution)/shard_map/attention_backward/pallas_call | solution.py:589
  89.7 0.0 copy-start.1
  89.7 1.6 %copy.12 = bf16[1,128,512]{2,1,0:T(8,128)(2,1)} copy(bf16[1,128,512]{2,1,0:T(8,128)(2,1)} %get-tuple-element.6) | data formatting | bytes 262144
  91.3 0.0 copy-done.1
  91.3 0.0 copy-start
  91.3 0.6 copy.13
  91.9 0.2 copy-done
  92.1 0.6 copy.14
Async XLA Ops:
  89.7 1.6 %copy-start.1 = (bf16[1,128,128]{2,1,0:T(8,128)(2,1)S(1)}, bf16[1,128,128]{2,1,0:T(8,128)(2,1)}, u32[]{:S(2)}) copy-start(bf16[1,128,128]{2,1,0:T(8,128)(2,1)} %get-tuple-element.7) | copy-start | bytes 98308
  91.3 0.8 copy-start

commit v2 on v1

v2 whole, which is shorter than its diff:
```python
import functools

import jax
import jax.numpy as jnp
from jax import lax
from jax.experimental import pallas as pl
from jax.experimental.pallas import tpu as pltpu
from jax.sharding import PartitionSpec as P

MESH = pl.DeviceIdType.MESH
F32 = jnp.float32
BF16 = jnp.bfloat16

NZ = 8
NX = 4
NT = 4
HEADS = 4
HALF = 64
HD = 128
ROW = 2 * NX
ROWS = HEADS * HALF
KEYS = ROW * HALF
INV_ROOT = HD ** (-0.5)
LOG2E = 1.4426950408889634
NEG = -1e30
POS = 1e30
ORDER = (0, 1, -1, 2, -2, 3, -3, 4)
ACROSS = (0, 1, 3, 2)
SETS = ((0, 1), (3, 2))


def dot_nt(a, b):
    return lax.dot_general(a, b, (((1,), (1,)), ((), ())), preferred_element_type=F32)


def dot_nn(a, b):
    return jnp.dot(a, b, preferred_element_type=F32)


def dot_tn(a, b):
    return lax.dot_general(a, b, (((0,), (0,)), ((), ())), preferred_element_type=F32)


def col_sum(v):
    return jnp.sum(v, axis=0, keepdims=True)


def col_max(v):
    return jnp.max(v, axis=0, keepdims=True)


def kernel(
    q_ref, k_ref, v_ref, g_ref, span_ref,
    dq_out, dk_out, dv_out,
    kbuf, vbuf, s1, s2, dp1, dp2, kselbuf, qq, oo, dql, dq2, dqst, state, tops, diag,
    pk, pv, sib, rr, cr1, cr2, zr, xr, ysum, yr,
    p1ks, p1kr, p1vs, p1vr, zks, zkr, zvs, zvr, x1s, x1r, x2s, x2r, d2ds, d2dr,
    sibs, sibr, rs, rrsem, c1s, c1r, c2s, c2r, zs, zrsem, xs, xrsem, ys, yrsem, dqsem,
):
    pipe = lax.axis_index("pipe")
    me = lax.axis_index("ctx")
    t = lax.axis_index("tp")
    z = me // (2 * NX)
    x = (me // 2) % NX
    c = me % 2

    def at(zz, xx, cc):
        return (pipe, (zz * NX + xx) * 2 + cc, t)

    def zoff(d):
        return lax.rem(z + d + NZ, NZ)

    def xoff(d):
        return lax.rem(x + d + NX, NX)

    def row_of(n):
        return zoff(((n + 1) // 2) * (2 * (n % 2) - 1))

    def other(tt, cc):
        return (1 - pipe, (z * NX + x) * 2 + cc, tt)

    sibling = at(z, x, 1 - c)

    def remote(src, dst, ssem, rsem, dev):
        return pltpu.make_async_remote_copy(
            src_ref=src, dst_ref=dst, send_sem=ssem, recv_sem=rsem,
            device_id=dev, device_id_type=MESH,
        )

    barrier = pltpu.get_barrier_semaphore()
    count = 0

    def greet(dev):
        pl.semaphore_signal(barrier, inc=1, device_id=dev, device_id_type=MESH)

    greet(sibling)
    count += 1
    for cc in range(2):
        for d in range(1, NX):
            greet(at(z, xoff(d), cc))
            count += 1
        for d in (1, -1, 2, -2):
            greet(at(zoff(d), x, cc))
            count += 1
        for tt in range(NT):
            greet(other(tt, cc))
            count += 1

    for h in range(HEADS):
        cols = slice(h * HD, (h + 1) * HD)
        rows = slice(h * HALF, (h + 1) * HALF)
        qq[rows, 0:HD] = q_ref[0, 0:HALF, cols]
        qq[rows, HD:2 * HD] = q_ref[0, HALF:2 * HALF, cols]
        oo[rows, 0:HD] = g_ref[0, 0:HALF, cols]
        oo[rows, HD:2 * HD] = g_ref[0, HALF:2 * HALF, cols]

    scale = INV_ROOT * LOG2E
    key_no = lax.broadcasted_iota(jnp.int32, (HALF, ROWS), 0)
    tok_no = lax.broadcasted_iota(jnp.int32, (HALF, ROWS), 1) % HALF
    seen = key_no <= tok_no
    for j in range(2):
        half = slice(j * HALF, (j + 1) * HALF)
        cols = slice(j * HD, (j + 1) * HD)
        s = jnp.where(seen, dot_nt(k_ref[0, half], qq[:, cols]) * scale, NEG)
        top = col_max(s)
        p = jnp.exp2(s - top)
        dp = dot_nt(v_ref[0, half], oo[:, cols])
        diag[2 * j] = p
        diag[2 * j + 1] = dp
        state[j:j + 1] = top
        state[2 + j:3 + j] = col_sum(p)
        state[4 + j:5 + j] = col_sum(p * dp)
        tops[NZ, j:j + 1] = top

    pl.semaphore_wait(barrier, count)

    def first_k(d):
        return remote(k_ref.at[0], kbuf.at[z, x, c], p1ks.at[d], p1kr.at[d, c], at(z, xoff(d), 0))

    def first_v(i):
        return remote(v_ref.at[0], vbuf.at[z, x, c], p1vs.at[i], p1vr.at[i, c],
                      at(zoff((0, 1, -1, 2, -2)[i]), x, 1))

    def k_send(way, k, j):
        step = 1 if way == 0 else -1
        ref = kbuf.at[zoff(-step * (k - 1)), xoff(j)]
        return remote(ref, ref, zks.at[way, k - 1, j], zkr.at[way, k - 1, j], at(zoff(step), x, 0))

    def v_far(way, k):
        step = 1 if way == 0 else -1
        if k == 3:
            ref = vbuf.at[zoff(-2 * step), x]
        else:
            ref = vbuf.at[zoff(-2 * step), x, way]
        return remote(ref, ref, zvs.at[way, k - 3], zvr.at[way, k - 3],
                      at(zoff(step * (k - 2)), x, 1))

    def v_x1(way, n):
        step = 1 if way == 0 else -1
        ref = vbuf.at[zoff(ORDER[n]), x]
        return remote(ref, ref, x1s.at[way, n], x1r.at[way, n], at(z, xoff(step), 1))

    def v_x2(way, n):
        step = 1 if way == 0 else -1
        ref = vbuf.at[zoff(ORDER[n]), xoff(-step), way]
        return remote(ref, ref, x2s.at[way, n], x2r.at[way, n], at(z, xoff(step), 1))

    def hand_over(buf, n):
        ref = buf.at[row_of(n)]
        return remote(ref, ref, d2ds.at[n], d2dr.at[n], sibling)

    def landed(sem):
        pltpu.make_async_copy(kbuf.at[0, 0, 0], kbuf.at[0, 0, 0], sem).wait()

    def gather_k(n):
        d = ORDER[n]
        k = abs(d)
        if k == 0:
            for j in ACROSS:
                src = (NX - j) % NX
                for cc in range(2):
                    if (src, cc) != (0, 0):
                        landed(p1kr.at[src, cc])
                for w in range(2):
                    k_send(w, 1, j).start()
        elif k < 4:
            w = 1 if d > 0 else 0
            for j in ACROSS:
                k_send(w, k, j).wait_recv()
                if k < 3 or j in SETS[w]:
                    k_send(w, k + 1, j).start()
        else:
            for w in range(2):
                for j in SETS[w]:
                    k_send(w, 4, j).wait_recv()
        hand_over(kbuf, n).start()

    def v_stage1(n):
        d = ORDER[n]
        if d == 0:
            landed(p1vr.at[0, 0])
        elif abs(d) <= 2:
            i = (0, 1, -1, 2, -2).index(-d)
            for cc in range(2):
                landed(p1vr.at[i, cc])
            if abs(d) == 2:
                w = 1 if d > 0 else 0
                v_far(w, 3).start()
                v_far(w, 4).start()
        elif abs(d) == 3:
            v_far(1 if d > 0 else 0, 3).wait_recv()
        else:
            v_far(0, 4).wait_recv()
            v_far(1, 4).wait_recv()
        for w in range(2):
            v_x1(w, n).start()

    def v_stage2(n):
        for w in range(2):
            v_x1(w, n).wait_recv()
            v_x2(w, n).start()

    def v_stage3(n):
        for w in range(2):
            v_x2(w, n).wait_recv()
        hand_over(vbuf, n).start()

    for d in (1, 3, 2):
        first_k(d).start()

    @pl.when(c == 1)
    def _():
        first_k(0).start()
        vbuf[z, x, 1] = v_ref[0]

    @pl.when(c == 0)
    def _():
        first_v(0).start()
        kbuf[z, x, 0] = k_ref[0]

    for i in (3, 4, 1, 2):
        first_v(i).start()

    my_block = span_ref[0, me, 0]

    def early(b, i):
        return span_ref[0, b * ROW + i, 0] < my_block

    def pick(buf, b):
        e, both = [], []
        for i in range(ROW):
            blk = buf[b, i // 2, i % 2]
            lo, hi = blk[:HALF], blk[HALF:]
            s = early(b, i)
            zero = jnp.zeros_like(lo)
            e.append(lo)
            both.append(jnp.concatenate([jnp.where(s, lo, zero), jnp.where(s, zero, hi)], axis=1))
        return jnp.concatenate(e, axis=0), jnp.concatenate(both, axis=0)

    def softmax_row(n):
        b = row_of(n)

        @pl.when(c == 0)
        def _():
            hand_over(vbuf, n).wait_recv()

        @pl.when(c == 1)
        def _():
            hand_over(kbuf, n).wait_recv()

        ke, ksel = pick(kbuf, b)
        kselbuf[b] = ksel
        s1[b] = dot_nt(ke, qq[:, HD:]) * scale
        s2[b] = dot_nt(ksel, qq[...]) * scale
        ve, vsel = pick(vbuf, b)
        dp1[b] = dot_nt(ve, oo[:, HD:])
        dp2[b] = dot_nt(vsel, oo[...])
        old_e, old_l = state[0:1], state[1:2]
        m_e, m_l = old_e, jnp.maximum(old_l, col_max(s1[b]))
        low = jnp.full((1, ROWS), NEG, F32)
        high = jnp.full((1, ROWS), POS, F32)
        for i in range(ROW):
            top = col_max(s2[b, i * HALF:(i + 1) * HALF])
            s = early(b, i)
            top = jnp.where(b * ROW + i == me, low, top)
            m_e = jnp.maximum(m_e, jnp.where(s, top, low))
            m_l = jnp.maximum(m_l, jnp.where(s, low, top))
        a_e = jnp.exp2(old_e - m_e)
        a_l = jnp.exp2(old_l - m_l)
        l_e, l_l = state[2:3] * a_e, state[3:4] * a_l
        d_e, d_l = state[4:5] * a_e, state[5:6] * a_l
        for i in range(ROW):
            part = slice(i * HALF, (i + 1) * HALF)
            p = jnp.exp2(s1[b, part] - m_l)
            s1[b, part] = p
            l_l = l_l + col_sum(p)
            d_l = d_l + col_sum(p * dp1[b, part])
            s = early(b, i)
            top = jnp.where(s, m_e, m_l)
            top = jnp.where(b * ROW + i == me, high, top)
            p = jnp.exp2(s2[b, part] - top)
            s2[b, part] = p
            ps = col_sum(p)
            pd = col_sum(p * dp2[b, part])
            zero = jnp.zeros_like(ps)
            l_e = l_e + jnp.where(s, ps, zero)
            l_l = l_l + jnp.where(s, zero, ps)
            d_e = d_e + jnp.where(s, pd, zero)
            d_l = d_l + jnp.where(s, zero, pd)
        for i, v in enumerate((m_e, m_l, l_e, l_l, d_e, d_l)):
            state[i:i + 1] = v
        tops[b, 0:1] = m_e
        tops[b, 1:2] = m_l

    LAG = 3
    core0 = {i: (lambda i=i: gather_k(i)) for i in range(NZ)}
    core1_plan = {
        0: ((v_stage1, 0), (v_stage1, 1), (v_stage1, 2)),
        1: ((v_stage1, 3), (v_stage1, 4), (v_stage2, 0)),
        2: ((v_stage2, 1), (v_stage2, 2), (v_stage3, 0)),
        3: ((v_stage1, 5), (v_stage1, 6), (v_stage1, 7), (v_stage3, 1), (v_stage3, 2)),
        4: ((v_stage2, 3), (v_stage2, 4)),
        5: ((v_stage3, 3), (v_stage3, 4), (v_stage2, 5), (v_stage2, 6), (v_stage2, 7)),
        6: ((v_stage3, 5), (v_stage3, 6), (v_stage3, 7)),
    }

    def gather_step(i, _):
        for j in range(NZ):
            @pl.when((i == j) & (c == 0))
            def _():
                core0[j]()

            if j in core1_plan:
                @pl.when((i == j) & (c == 1))
                def _():
                    for stage, n in core1_plan[j]:
                        stage(n)

        @pl.when(i >= LAG)
        def _():
            softmax_row(i - LAG)

        return 0

    lax.fori_loop(0, NZ + LAG, gather_step, 0)

    m_e, m_l = state[0:1], state[1:2]
    r_e, r_l = 1.0 / state[2:3], 1.0 / state[3:4]
    d_e, d_l = state[4:5] * r_e, state[5:6] * r_l

    own_k, own_v = [], []
    for j, (m, r, d) in enumerate(((m_e, r_e, d_e), (m_l, r_l, d_l))):
        half = slice(j * HALF, (j + 1) * HALF)
        cols = slice(j * HD, (j + 1) * HD)
        p = diag[2 * j] * (jnp.exp2(tops[NZ, j:j + 1] - m) * r)
        ds = (p * (diag[2 * j + 1] - d)).astype(BF16)
        own_k.append(dot_nn(ds, qq[:, cols]) * INV_ROOT)
        own_v.append(dot_nn(p.astype(BF16), oo[:, cols]))
        dq2[cols] = dot_tn(k_ref[0, half], ds)
    for j in range(2):
        diag[j, :, :HD] = own_k[j]
        diag[j, :, HD:] = own_v[j]
    dql[...] = jnp.zeros_like(dql)
    state[2:3] = r_e
    state[3:4] = r_l
    state[4:5] = d_e
    state[5:6] = d_l

    def give(buf, m):
        b = row_of(NZ - 1 - m)
        return remote(buf.at[b], sib.at[b], sibs.at[m], sibr.at[m], sibling)

    def gradient_row(m):
        b = row_of(NZ - 1 - m)
        r_e, r_l, d_e, d_l = state[2:3], state[3:4], state[4:5], state[5:6]
        f_e = jnp.exp2(tops[b, 0:1] - state[0:1]) * r_e
        f_l = jnp.exp2(tops[b, 1:2] - state[1:2]) * r_l
        ke = jnp.concatenate([kbuf[b, i // 2, i % 2, :HALF] for i in range(ROW)], axis=0)
        ksel = kselbuf[b]
        p1 = s1[b] * f_l
        ds1 = (p1 * (dp1[b] - d_l)).astype(BF16)
        p1 = p1.astype(BF16)
        p2s, ds2s = [], []
        for i in range(ROW):
            part = slice(i * HALF, (i + 1) * HALF)
            s = early(b, i)
            p = s2[b, part] * jnp.where(s, f_e, f_l)
            ds2s.append((p * (dp2[b, part] - jnp.where(s, d_e, d_l))).astype(BF16))
            p2s.append(p.astype(BF16))
        p2 = jnp.concatenate(p2s, axis=0)
        ds2 = jnp.concatenate(ds2s, axis=0)
        v1 = dot_nn(p1, oo[:, HD:])
        v2 = dot_nn(p2, oo[...])
        k1 = dot_nn(ds1, qq[:, HD:]) * INV_ROOT
        k2 = dot_nn(ds2, qq[...]) * INV_ROOT
        dql[...] += dot_tn(ke, ds1)
        dq2[...] += dot_tn(ksel, ds2)
        for i in range(ROW):
            part = slice(i * HALF, (i + 1) * HALF)
            s = early(b, i)
            zero = jnp.zeros((HALF, HD), F32)
            cell = (b, i // 2, i % 2)
            lo, hi = slice(0, HALF), slice(HALF, 2 * HALF)
            pv[(*cell, lo)] = (v1[part] + jnp.where(s, v2[part, :HD], zero)).astype(BF16)
            pv[(*cell, hi)] = jnp.where(s, zero, v2[part, HD:]).astype(BF16)
            pk[(*cell, lo)] = (k1[part] + jnp.where(s, k2[part, :HD], zero)).astype(BF16)
            pk[(*cell, hi)] = jnp.where(s, zero, k2[part, HD:]).astype(BF16)

        @pl.when(m == NZ - 1)
        def _():
            for j in range(2):
                half = slice(j * HALF, (j + 1) * HALF)
                pk[z, x, c, half] = (pk[z, x, c, half].astype(F32) + diag[j, :, :HD]).astype(BF16)
                pv[z, x, c, half] = (pv[z, x, c, half].astype(F32) + diag[j, :, HD:]).astype(BF16)

        @pl.when(c == 0)
        def _():
            give(pv, m).start()

        @pl.when(c == 1)
        def _():
            give(pk, m).start()

    def add_into(dst, idx, *terms):
        total = dst[idx].astype(F32)
        for ref, i in terms:
            total = total + ref[i].astype(F32)
        dst[idx] = total.astype(BF16)

    def k_back(way, k, j):
        step = 1 if way == 0 else -1
        return remote(pk.at[zoff(step * k), xoff(j)], rr.at[way, k - 1, j],
                      rs.at[way, k - 1, j], rrsem.at[way, k - 1, j], at(zoff(step), x, 0))

    def k_across(j):
        return remote(pk.at[z, xoff(j)], xr.at[j], xs.at[j], xrsem.at[j], at(z, xoff(j), 0))

    def k_hop(m):
        give(pk, m).wait_recv()
        d = ORDER[NZ - 1 - m]
        k = abs(d)
        if k == 4:
            plan = [(w, j, False) for i in range(2) for w, j in ((0, SETS[0][i]), (1, SETS[1][i]))]
        else:
            w = 0 if d > 0 else 1
            plan = [(w, j, k < 3 or j in SETS[w]) for j in SETS[1 - w] + SETS[w]]
        for w, j, has in plan:
            cell = (zoff(d), xoff(j))
            terms = [(sib, cell)]
            if has:
                k_back(w, k + 1, j).wait_recv()
                terms.append((rr, (w, k, j)))
            add_into(pk, cell, *terms)
            k_back(w, k, j).start()

    def k_last():
        give(pk, NZ - 1).wait_recv()
        for j in (2, 1, 3, 0):
            for w in range(2):
                k_back(w, 1, j).wait_recv()
            cell = (z, xoff(j))
            add_into(pk, cell, (sib, cell), (rr, (0, 0, j)), (rr, (1, 0, j)))
            if j:
                k_across(j).start()
        total = pk[z, x].astype(F32)
        for j in range(1, NX):
            k_across(j).wait_recv()
            total = total + xr[j].astype(F32)
        ysum[...] = total.astype(BF16)

    def v_back2(way, m):
        step = 1 if way == 0 else -1
        return remote(pv.at[zoff(ORDER[NZ - 1 - m]), xoff(2), way], cr2.at[way, m],
                      c2s.at[way, m], c2r.at[way, m], at(z, xoff(step), 1))

    def v_back1(way, m):
        step = 1 if way == 0 else -1
        return remote(pv.at[zoff(ORDER[NZ - 1 - m]), xoff(step)], cr1.at[way, m],
                      c1s.at[way, m], c1r.at[way, m], at(z, xoff(step), 1))

    def v_z(way, k):
        step = 1 if way == 0 else -1
        if k == 4:
            src, dst, far = pv.at[zoff(4), x, way], zr.at[way, 3, way], 2
        else:
            src, dst, far = pv.at[zoff(step * k), x], zr.at[way, k - 1], (1, 2, 1)[k - 1]
        return remote(src, dst, zs.at[way, k - 1], zrsem.at[way, k - 1], at(zoff(step * far), x, 1))

    def v_hop2(m):
        give(pv, m).wait_recv()
        for w in range(2):
            cell = (zoff(ORDER[NZ - 1 - m]), xoff(2), w)
            add_into(pv, cell, (sib, cell))
            v_back2(w, m).start()

    def v_hop1(m):
        for w in range(2):
            row = zoff(ORDER[NZ - 1 - m])
            col = xoff(1 if w == 0 else -1)
            add_into(pv, (row, col, 1 - w), (sib, (row, col, 1 - w)))
            v_back2(w, m).wait_recv()
            add_into(pv, (row, col, w), (sib, (row, col, w)), (cr2, (w, m)))
            v_back1(w, m).start()

    def v_hop0(m):
        d = ORDER[NZ - 1 - m]
        k = abs(d)
        w = 0 if d > 0 else 1
        cell = (zoff(d), x)
        for ww in range(2):
            v_back1(ww, m).wait_recv()
        terms = [(sib, cell), (cr1, (0, m)), (cr1, (1, m))]
        if k == 2:
            v_z(w, 3).wait_recv()
            terms.append((zr, (w, 2)))
        add_into(pv, cell, *terms)
        if k == 2:
            v_z(w, 4).wait_recv()
            add_into(pv, (*cell, w), (zr, (w, 3, w)))
        if k == 4:
            v_z(0, 4).start()
            v_z(1, 4).start()
        elif k > 0:
            v_z(w, k).start()

    def v_last():
        total = pv[z, x].astype(F32)
        for k in (1, 2):
            for w in range(2):
                v_z(w, k).wait_recv()
                total = total + zr[w, k - 1].astype(F32)
        ysum[...] = total.astype(BF16)

    back0 = {2: ((k_hop, 0),), 5: ((k_hop, 1),), 6: ((k_hop, 2),)}
    back1 = {m: ((v_hop2, m - 2),) + (((v_hop1, m - 5),) if m >= 5 else ()) for m in range(2, NZ)}

    def scatter_step(m, _):
        gradient_row(m)
        for j in range(NZ):
            for core, plan in ((0, back0), (1, back1)):
                if j in plan:
                    @pl.when((m == j) & (c == core))
                    def _():
                        for stage, n in plan[j]:
                            stage(n)
        return 0

    lax.fori_loop(0, NZ, scatter_step, 0)

    @pl.when(c == 0)
    def _():
        k_hop(3)

    @pl.when(c == 1)
    def _():
        v_hop2(6)
        v_hop2(7)
        v_hop1(3)
        v_hop1(4)

    for j, acc in enumerate((dq2[0:HD], dq2[HD:2 * HD] + dql[...])):
        g = (acc * INV_ROOT).T.astype(BF16)
        for h in range(HEADS):
            dqst[j * HALF:(j + 1) * HALF, h * HD:(h + 1) * HD] = g[h * HALF:(h + 1) * HALF]
    dq_copy = remote(dqst, dq_out.at[0], dqsem.at[0], dqsem.at[1], other(t, c))
    dq_copy.start()

    @pl.when(c == 0)
    def _():
        for m in (4, 5, 6):
            k_hop(m)
        k_last()

    @pl.when(c == 1)
    def _():
        v_hop0(0)
        v_hop0(1)
        v_hop0(2)
        v_hop1(5)
        v_hop1(6)
        v_hop1(7)
        for m in range(3, NZ):
            v_hop0(m)
        v_last()

    def last(tt, cc):
        i = tt * 2 + cc
        return remote(ysum.at[cc], yr.at[c, t], ys.at[i], yrsem.at[c, t], other(tt, cc))

    for tt in range(NT):
        for cc in range(2):
            last(tt, cc).start()

    @pl.when(c == 0)
    def _():
        first_v(0).wait_send()
        for w in range(2):
            for k in range(1, 5):
                for j in range(NX):
                    if k < 4 or j in SETS[w]:
                        k_send(w, k, j).wait_send()
                        k_back(w, k, j).wait_send()
        for n in range(NZ):
            hand_over(kbuf, n).wait_send()
            give(pv, n).wait_send()
        for j in range(1, NX):
            k_across(j).wait_send()

    @pl.when(c == 1)
    def _():
        first_k(0).wait_send()
        for w in range(2):
            for n in range(NZ):
                v_x1(w, n).wait_send()
                v_x2(w, n).wait_send()
                v_back1(w, n).wait_send()
                v_back2(w, n).wait_send()
            for k in (3, 4):
                v_far(w, k).wait_send()
            for k in range(1, 5):
                v_z(w, k).wait_send()
        for n in range(NZ):
            hand_over(vbuf, n).wait_send()
            give(pk, n).wait_send()

    for d in range(1, NX):
        first_k(d).wait_send()
    for i in range(1, 5):
        first_v(i).wait_send()

    for kind, out in ((0, dk_out), (1, dv_out)):
        total = jnp.zeros((128, HD), F32)
        for tt in range(NT):
            landed(yrsem.at[kind, tt])
            total = total + yr[kind, tt].astype(F32)
        out[0] = total.astype(BF16)
    for tt in range(NT):
        for cc in range(2):
            last(tt, cc).wait_send()
    dq_copy.wait()


def per_device(queries, keys, values, grad_out, span_order):
    vmem = pl.BlockSpec(memory_space=pltpu.VMEM)
    dma = pltpu.SemaphoreType.DMA

    def plane():
        return pltpu.VMEM((NZ, NX, 2, 128, HD), BF16)

    scratch = [
        plane(),
        plane(),
        pltpu.VMEM((NZ, KEYS, ROWS), F32),
        pltpu.VMEM((NZ, KEYS, ROWS), F32),
        pltpu.VMEM((NZ, KEYS, ROWS), F32),
        pltpu.VMEM((NZ, KEYS, ROWS), F32),
        pltpu.VMEM((NZ, KEYS, 2 * HD), BF16),
        pltpu.VMEM((ROWS, 2 * HD), BF16),
        pltpu.VMEM((ROWS, 2 * HD), BF16),
        pltpu.VMEM((HD, ROWS), F32),
        pltpu.VMEM((2 * HD, ROWS), F32),
        pltpu.VMEM((128, HEADS * HD), BF16),
        pltpu.VMEM((8, ROWS), F32),
        pltpu.VMEM((NZ + 1, 8, ROWS), F32),
        pltpu.VMEM((4, HALF, ROWS), F32),
        plane(),
        plane(),
        plane(),
        pltpu.VMEM((2, 4, NX, 2, 128, HD), BF16),
        pltpu.VMEM((2, NZ, 2, 128, HD), BF16),
        pltpu.VMEM((2, NZ, 128, HD), BF16),
        pltpu.VMEM((2, 4, 2, 128, HD), BF16),
        pltpu.VMEM((NX, 2, 128, HD), BF16),
        pltpu.VMEM((2, 128, HD), BF16),
        pltpu.VMEM((2, NT, 128, HD), BF16),
        dma((NX,)), dma((NX, 2)), dma((5,)), dma((5, 2)),
        dma((2, 4, NX)), dma((2, 4, NX)), dma((2, 2)), dma((2, 2)),
        dma((2, NZ)), dma((2, NZ)), dma((2, NZ)), dma((2, NZ)),
        dma((NZ,)), dma((NZ,)),
        dma((NZ,)), dma((NZ,)),
        dma((2, 4, NX)), dma((2, 4, NX)),
        dma((2, NZ)), dma((2, NZ)), dma((2, NZ)), dma((2, NZ)),
        dma((2, 4)), dma((2, 4)), dma((NX,)), dma((NX,)),
        dma((8,)), dma((2, NT)), dma((2,)),
    ]
    return pl.pallas_call(
        kernel,
        out_shape=(
            jax.ShapeDtypeStruct(queries.shape, BF16),
            jax.ShapeDtypeStruct(keys.shape, BF16),
            jax.ShapeDtypeStruct(values.shape, BF16),
        ),
        in_specs=[vmem, vmem, vmem, vmem, pl.BlockSpec(memory_space=pltpu.SMEM)],
        out_specs=(pl.BlockSpec(memory_space=pl.ANY), vmem, vmem),
        scratch_shapes=scratch,
        compiler_params=pltpu.CompilerParams(
            collective_id=1, has_side_effects=True, vmem_limit_bytes=56 * 2**20
        ),
        name="attention_backward",
    )(queries, keys, values, grad_out, span_order)


def solution(mesh):
    return jax.shard_map(
        per_device,
        mesh=mesh,
        in_specs=(
            P("pipe", "ctx", "tp"),
            P("pipe", "ctx", None),
            P("pipe", "ctx", None),
            P("pipe", "ctx", "tp"),
            P("pipe", None, None),
        ),
        out_specs=(P("pipe", "ctx", "tp"), P("pipe", "ctx", None), P("pipe", "ctx", None)),
        check_vma=False,
    )
```

time: 93 us -> 82.5 us (0.89)
  Pallas kernels: 87.7 us -> 77.2 us
    pallas_call x1, Pallas kernels: 87.7 us -> 77.2 us  [per_device(): pl.pallas_call(kernel, out_shape=(jax.ShapeDtypeStruct(queries.shape, BF1...]
where the time goes in v2:
time: 82.5 us; the launch traced here: 82.2 us
  Pallas kernels  77.2 us (94%)
  local copies, waits for them, and re-layouts  4.34 us (5%)
    pallas_call x1, Pallas kernels, per_device(): pl.pallas_call(kernel, out_shape=(jax.ShapeDtypeStruct(queries.shape, BF1...  77.2 us
    unnamed x8, local copies, waits for them, and re-layouts  4.34 us

profile of v2, /device:TPU:1, one launch (start us, length us, event | category | flops | bytes accessed | tf_op | source)
XLA Modules:
  0.0 82.2 jit_solution(3766955413014741056)
XLA Ops:
  0.6 1.4 %copy.8.span_ref = s32[1,64,2]{2,1,0:T(8,128)} copy(s32[1,64,2]{1,2,0:T(2,128)} %param.9) | data formatting | bytes 1024 | tf_op args[4]
  2.0 77.2 %attention_backward.1 = (bf16[1,128,512]{2,1,0:T(8,128)(2,1)}, bf16[1,128,128]{2,1,0:T(8,128)(2,1)}, bf16[1,128,128]{2,1,0:T(8,128)(2,1)}) custom-call(bf16[1,128,512]{2,1,0:T(8,128)(2,1)} %q_ref.1, bf16[1,128,128]{2,1,0:T(8,128)(2,1)} %k_ref.1, bf16[1,128,128]{2,1,0:T(8,128)(2,1)} %v_ref.1, bf16[1,128,512]{2,1,0:T(8,128)(2,1)} %g_ref.1, ...), custom_call_target="tpu_custom_call" | custom-call | tf_op jit(solution)/shard_map/attention_backward/pallas_call | solution.py:686
  79.2 0.0 copy-start.1
  79.2 1.6 %copy.12 = bf16[1,128,512]{2,1,0:T(8,128)(2,1)} copy(bf16[1,128,512]{2,1,0:T(8,128)(2,1)} %get-tuple-element.6) | data formatting | bytes 262144
  80.8 0.0 copy-done.1
  80.8 0.0 copy-start
  80.8 0.6 copy.13
  81.4 0.2 copy-done
  81.6 0.6 copy.14
Async XLA Ops:
  79.2 1.6 %copy-start.1 = (bf16[1,128,128]{2,1,0:T(8,128)(2,1)S(1)}, bf16[1,128,128]{2,1,0:T(8,128)(2,1)}, u32[]{:S(2)}) copy-start(bf16[1,128,128]{2,1,0:T(8,128)(2,1)} %get-tuple-element.7) | copy-start | bytes 98308
  80.8 0.8 copy-start

commit v3 on v2

v3 whole, which is shorter than its diff:
```python
import functools

import jax
import jax.numpy as jnp
from jax import lax
from jax.experimental import pallas as pl
from jax.experimental.pallas import tpu as pltpu
from jax.sharding import PartitionSpec as P

MESH = pl.DeviceIdType.MESH
F32 = jnp.float32
BF16 = jnp.bfloat16

NZ = 8
NX = 4
NT = 4
HEADS = 4
HALF = 64
HD = 128
ROWS = HEADS * HALF
SLOTS = 2 * ROWS
KEYS = NX * HALF
INV_ROOT = HD ** (-0.5)
LOG2E = 1.4426950408889634
NEG = -1e30
POS = 1e30
ORDER = (0, 1, -1, 2, -2, 3, -3, 4)
ACROSS = (0, 1, 3, 2)
SETS = ((0, 1), (3, 2))


def dot_nt(a, b):
    return lax.dot_general(a, b, (((1,), (1,)), ((), ())), preferred_element_type=F32)


def dot_nn(a, b):
    return jnp.dot(a, b, preferred_element_type=F32)


def dot_tn(a, b):
    return lax.dot_general(a, b, (((0,), (0,)), ((), ())), preferred_element_type=F32)


def col_sum(v):
    return jnp.sum(v, axis=0, keepdims=True)


def col_max(v):
    return jnp.max(v, axis=0, keepdims=True)


def kernel(
    q_ref, k_ref, v_ref, g_ref, span_ref,
    dq_out, dk_out, dv_out,
    kbuf, vbuf, s1, s2, dp1, dp2, kselbuf, qq, oo, pq, pg, dql, dq2, dqst, dqr,
    state, tops, diag, sums_out, sums_in,
    pk, pv, sib, rr, cx, zr, xr, ysum, yr,
    p1ks, p1kr, p1vs, p1vr, zks, zkr, x1s, x1r, d2ds, d2dr,
    pqs, pqr, sums_s, sums_r, sibs, sibr, rs, rrsem, c1s, c1r, zs, zrsem, xs, xrsem, ys, yrsem, dqs, dqsr,
):
    pipe = lax.axis_index("pipe")
    me = lax.axis_index("ctx")
    t = lax.axis_index("tp")
    z = me // (2 * NX)
    x = (me // 2) % NX
    c = me % 2
    half = t % 2
    mates = (t + 1 - 2 * half, lax.rem(t + 2 * half + NT - 1, NT))

    def at(zz, xx, cc):
        return (pipe, (zz * NX + xx) * 2 + cc, t)

    def zoff(d):
        return lax.rem(z + d + NZ, NZ)

    def xoff(d):
        return lax.rem(x + d + NX, NX)

    def row_of(n):
        return zoff(((n + 1) // 2) * (2 * (n % 2) - 1))

    def mate(j):
        return (pipe, me, mates[j])

    def other(tt, cc):
        return (1 - pipe, (z * NX + x) * 2 + cc, tt)

    sibling = at(z, x, 1 - c)

    def remote(src, dst, ssem, rsem, dev):
        return pltpu.make_async_remote_copy(
            src_ref=src, dst_ref=dst, send_sem=ssem, recv_sem=rsem,
            device_id=dev, device_id_type=MESH,
        )

    barrier = pltpu.get_barrier_semaphore()
    count = 0

    def greet(dev):
        pl.semaphore_signal(barrier, inc=1, device_id=dev, device_id_type=MESH)

    greet(sibling)
    count += 1
    for cc in range(2):
        for d in range(1, NX):
            greet(at(z, xoff(d), cc))
            count += 1
        for d in range(1, NZ):
            greet(at(zoff(d), x, cc))
            count += 1
        for tt in range(NT):
            greet(other(tt, cc))
            count += 1
    for j in range(2):
        greet(mate(j))
        count += 1

    def lay_rows(dst, base, src, lo, j):
        for h in range(HEADS):
            dst[base + h * HALF:base + (h + 1) * HALF, j * HD:(j + 1) * HD] = src[
                lo:lo + HALF, h * HD:(h + 1) * HD]

    for j in range(2):
        lay_rows(qq, 0, q_ref.at[0], j * HALF, j)
        lay_rows(oo, 0, g_ref.at[0], j * HALF, j)
    low = jnp.full((1, SLOTS), NEG, F32)
    state[...] = jnp.zeros_like(state)
    sums_out[...] = jnp.zeros_like(sums_out)
    for j in range(2):
        state[j:j + 1] = low
    dql[...] = jnp.zeros_like(dql)
    dq2[...] = jnp.zeros_like(dq2)
    scale = INV_ROOT * LOG2E

    pl.semaphore_wait(barrier, count)

    def swap_rows(j, kind):
        src = (q_ref, g_ref)[kind].at[0, pl.ds(j * HALF, HALF)]
        dst = (pq, pg)[kind].at[j]
        return remote(src, dst, pqs.at[j, kind], pqr.at[j, kind], mate(j))

    for kind in range(2):
        for j in range(2):
            swap_rows(j, kind).start()

    def first_k(d):
        return remote(k_ref.at[0], kbuf.at[z, x], p1ks.at[d], p1kr.at[d], at(z, xoff(d), 1))

    def first_v(d):
        return remote(v_ref.at[0], vbuf.at[z, x], p1vs.at[d], p1vr.at[d], at(zoff(d), x, 0))

    def k_send(way, k, j):
        step = 1 if way == 0 else -1
        back, far = (2, 2) if k == 4 else (k - 1, 1)
        ref = kbuf.at[zoff(-step * back), xoff(j)]
        return remote(ref, ref, zks.at[way, k - 1, j], zkr.at[way, k - 1, j],
                      at(zoff(step * far), x, 1))

    def v_x(d, n):
        ref = vbuf.at[zoff(ORDER[n]), x]
        return remote(ref, ref, x1s.at[d, n], x1r.at[d, n], at(z, xoff(d), 0))

    def hand_over(buf, n):
        ref = buf.at[row_of(n)]
        return remote(ref, ref, d2ds.at[n], d2dr.at[n], sibling)

    def landed(sem):
        pltpu.make_async_copy(kbuf.at[0, 0], kbuf.at[0, 0], sem).wait()

    def gather_k(n):
        d = ORDER[n]
        k = abs(d)
        if k == 0:
            for j in ACROSS:
                src = (NX - j) % NX
                if src:
                    landed(p1kr.at[src])
                else:
                    @pl.when(half == 0)
                    def _():
                        landed(p1kr.at[0])
                for w in range(2):
                    k_send(w, 1, j).start()
        elif k < 4:
            w = 1 if d > 0 else 0
            for j in ACROSS:
                k_send(w, k, j).wait_recv()
                if k == 1:
                    k_send(w, 2, j).start()
                if k == 2:
                    if j in SETS[w]:
                        k_send(w, 4, j).start()
                    k_send(w, 3, j).start()
        else:
            for w in range(2):
                for j in SETS[w]:
                    k_send(w, 4, j).wait_recv()
        hand_over(kbuf, n).start()

    def v_stage1(n):
        d = ORDER[n]
        if d:
            landed(p1vr.at[-d % NZ])
        else:
            @pl.when(half == 1)
            def _():
                landed(p1vr.at[0])
        for dx in (1, 3, 2):
            v_x(dx, n).start()

    def v_stage2(n):
        for dx in range(1, NX):
            v_x(dx, n).wait_recv()
        hand_over(vbuf, n).start()

    @pl.when(c == half)
    def _():
        for d in (1, 3, 2):
            first_k(d).start()

        @pl.when(c == 0)
        def _():
            first_k(0).start()
            vbuf[z, x] = v_ref[0]

        @pl.when(c == 1)
        def _():
            first_v(0).start()
            kbuf[z, x] = k_ref[0]

        for d in (1, 7, 2, 6, 3, 5, 4):
            first_v(d).start()

    def drain_gather():
        @pl.when(c == 1)
        def _():
            for w in range(2):
                for k in range(1, 5):
                    for j in range(NX):
                        if k < 4 or j in SETS[w]:
                            k_send(w, k, j).wait_send()
            for n in range(NZ):
                hand_over(kbuf, n).wait_send()

        @pl.when(c == 0)
        def _():
            for n in range(NZ):
                for dx in range(1, NX):
                    v_x(dx, n).wait_send()
                hand_over(vbuf, n).wait_send()

        @pl.when(c == half)
        def _():
            for d in range(1, NX):
                first_k(d).wait_send()
            for d in range(1, NZ):
                first_v(d).wait_send()

            @pl.when(c == 0)
            def _():
                first_k(0).wait_send()

            @pl.when(c == 1)
            def _():
                first_v(0).wait_send()

        for j in range(2):
            for kind in range(2):
                swap_rows(j, kind).wait_send()
            swap_sums(j).wait_send()

    my_block = span_ref[0, 0, me]

    def index(b, i):
        return (b * NX + i) * 2 + half

    def early(b, i):
        return span_ref[0, 0, index(b, i)] < my_block

    def pick(buf, b):
        e, both = [], []
        for i in range(NX):
            blk = buf[b, i]
            lo, hi = blk[:HALF], blk[HALF:]
            s = early(b, i)
            zero = jnp.zeros_like(lo)
            e.append(lo)
            both.append(jnp.concatenate([jnp.where(s, lo, zero), jnp.where(s, zero, hi)], axis=1))
        return jnp.concatenate(e, axis=0), jnp.concatenate(both, axis=0)

    def softmax_row(n):
        b = row_of(n)

        @pl.when(c == 1)
        def _():
            hand_over(vbuf, n).wait_recv()

        @pl.when(c == 0)
        def _():
            hand_over(kbuf, n).wait_recv()

        ke, ksel = pick(kbuf, b)
        kselbuf[b] = ksel
        s1[b] = dot_nt(ke, qq[:, HD:]) * scale
        s2[b] = dot_nt(ksel, qq[...]) * scale
        ve, vsel = pick(vbuf, b)
        dp1[b] = dot_nt(ve, oo[:, HD:])
        dp2[b] = dot_nt(vsel, oo[...])
        old_e, old_l = state[0:1], state[1:2]
        m_e, m_l = old_e, jnp.maximum(old_l, col_max(s1[b]))
        low = jnp.full((1, SLOTS), NEG, F32)
        high = jnp.full((1, SLOTS), POS, F32)
        for i in range(NX):
            top = col_max(s2[b, i * HALF:(i + 1) * HALF])
            s = early(b, i)
            top = jnp.where(index(b, i) == me, low, top)
            m_e = jnp.maximum(m_e, jnp.where(s, top, low))
            m_l = jnp.maximum(m_l, jnp.where(s, low, top))
        a_e = jnp.exp2(old_e - m_e)
        a_l = jnp.exp2(old_l - m_l)
        l_e, l_l = state[2:3] * a_e, state[3:4] * a_l
        d_e, d_l = state[4:5] * a_e, state[5:6] * a_l
        for i in range(NX):
            part = slice(i * HALF, (i + 1) * HALF)
            p = jnp.exp2(s1[b, part] - m_l)
            s1[b, part] = p
            l_l = l_l + col_sum(p)
            d_l = d_l + col_sum(p * dp1[b, part])
            s = early(b, i)
            top = jnp.where(s, m_e, m_l)
            top = jnp.where(index(b, i) == me, high, top)
            p = jnp.exp2(s2[b, part] - top)
            s2[b, part] = p
            ps = col_sum(p)
            pd = col_sum(p * dp2[b, part])
            zero = jnp.zeros_like(ps)
            l_e = l_e + jnp.where(s, ps, zero)
            l_l = l_l + jnp.where(s, zero, ps)
            d_e = d_e + jnp.where(s, pd, zero)
            d_l = d_l + jnp.where(s, zero, pd)
        for i, v in enumerate((m_e, m_l, l_e, l_l, d_e, d_l)):
            state[i:i + 1] = v
        tops[b, 0:1] = m_e
        tops[b, 1:2] = m_l

    def diagonal():
        key_no = lax.broadcasted_iota(jnp.int32, (HALF, SLOTS), 0)
        tok_no = lax.broadcasted_iota(jnp.int32, (HALF, SLOTS), 1) % HALF
        seen = key_no <= tok_no
        for j in range(2):
            part = slice(j * HALF, (j + 1) * HALF)
            cols = slice(j * HD, (j + 1) * HD)
            s = jnp.where(seen, dot_nt(k_ref[0, part], qq[:, cols]) * scale, NEG)
            top = col_max(s)
            p = jnp.exp2(s - top)
            dp = dot_nt(v_ref[0, part], oo[:, cols])
            diag[2 * j] = p
            diag[2 * j + 1] = dp
            state[j:j + 1] = top
            state[2 + j:3 + j] = col_sum(p)
            state[4 + j:5 + j] = col_sum(p * dp)
            tops[NZ, j:j + 1] = top

    def swap_sums(j):
        return remote(sums_out.at[j], sums_in.at[j], sums_s.at[j], sums_r.at[j], mate(j))

    LAG = 5
    plans = (
        {
            0: [(v_stage1, n) for n in range(5)],
            1: [(v_stage1, 5), (v_stage1, 6), (v_stage1, 7), (v_stage2, 0), (v_stage2, 1)],
            2: [(v_stage2, 2), (v_stage2, 3)],
            3: [(v_stage2, 4)],
            4: [(v_stage2, 5)],
            5: [(v_stage2, 6)],
            6: [(v_stage2, 7)],
        },
        {n: [(gather_k, n)] for n in range(NZ)},
    )

    def run_plan(i, plans):
        for core in range(2):
            for j, todo in plans[core].items():
                @pl.when((i == j) & (c == core))
                def _():
                    for stage, n in todo:
                        stage(n)

    def gather_step(i, _):
        run_plan(i, plans)

        @pl.when(i == LAG)
        def _():
            for kind in range(2):
                for j in range(2):
                    swap_rows(j, kind).wait_recv()
                    lay_rows((qq, oo)[kind], ROWS, (pq, pg)[kind].at[j], 0, j)

            @pl.when(c == half)
            def _():
                diagonal()

        @pl.when(i >= LAG)
        def _():
            softmax_row(i - LAG)

        return 0

    lax.fori_loop(0, NZ + LAG, gather_step, 0)

    for j in range(2):
        for i in range(3):
            sums_out[j, i:i + 1] = state[2 * i + j:2 * i + j + 1]
        swap_sums(j).start()
    for j in range(2):
        swap_sums(j).wait_recv()
        m, l, d = (state[2 * i + j:2 * i + j + 1] for i in range(3))
        m2, l2, d2 = (
            jnp.concatenate([sums_in[j, i:i + 1, ROWS:], sums_in[j, i:i + 1, :ROWS]], axis=1)
            for i in range(3)
        )
        top = jnp.maximum(m, m2)
        a, a2 = jnp.exp2(m - top), jnp.exp2(m2 - top)
        r = 1.0 / (l * a + l2 * a2)
        state[j:j + 1] = top
        state[2 + j:3 + j] = r
        state[4 + j:5 + j] = (d * a + d2 * a2) * r

    @pl.when(c == half)
    def _():
        for j in range(2):
            part = slice(j * HALF, (j + 1) * HALF)
            cols = slice(j * HD, (j + 1) * HD)
            m, r, d = state[j:j + 1], state[2 + j:3 + j], state[4 + j:5 + j]
            p = diag[2 * j] * (jnp.exp2(tops[NZ, j:j + 1] - m) * r)
            ds = (p * (diag[2 * j + 1] - d)).astype(BF16)
            dq2[cols] = dot_tn(k_ref[0, part], ds)
            diag[2 * j, :, :HD] = dot_nn(ds, qq[:, cols]) * INV_ROOT
            diag[2 * j, :, HD:2 * HD] = dot_nn(p.astype(BF16), oo[:, cols])

    def give(buf, m):
        b = row_of(NZ - 1 - m)
        return remote(buf.at[b], sib.at[b], sibs.at[m], sibr.at[m], sibling)

    def gradient_row(m):
        b = row_of(NZ - 1 - m)
        r_e, r_l, d_e, d_l = state[2:3], state[3:4], state[4:5], state[5:6]
        f_e = jnp.exp2(tops[b, 0:1] - state[0:1]) * r_e
        f_l = jnp.exp2(tops[b, 1:2] - state[1:2]) * r_l
        ke = jnp.concatenate([kbuf[b, i, :HALF] for i in range(NX)], axis=0)
        ksel = kselbuf[b]
        p1 = s1[b] * f_l
        ds1 = (p1 * (dp1[b] - d_l)).astype(BF16)
        p1 = p1.astype(BF16)
        p2s, ds2s = [], []
        for i in range(NX):
            part = slice(i * HALF, (i + 1) * HALF)
            s = early(b, i)
            p = s2[b, part] * jnp.where(s, f_e, f_l)
            ds2s.append((p * (dp2[b, part] - jnp.where(s, d_e, d_l))).astype(BF16))
            p2s.append(p.astype(BF16))
        p2 = jnp.concatenate(p2s, axis=0)
        ds2 = jnp.concatenate(ds2s, axis=0)
        v1 = dot_nn(p1, oo[:, HD:])
        v2 = dot_nn(p2, oo[...])
        k1 = dot_nn(ds1, qq[:, HD:]) * INV_ROOT
        k2 = dot_nn(ds2, qq[...]) * INV_ROOT
        dql[...] += dot_tn(ke, ds1)
        dq2[...] += dot_tn(ksel, ds2)
        for i in range(NX):
            part = slice(i * HALF, (i + 1) * HALF)
            s = early(b, i)
            zero = jnp.zeros((HALF, HD), F32)
            cell = (b, i)
            lo, hi = slice(0, HALF), slice(HALF, 2 * HALF)
            pv[(*cell, lo)] = (v1[part] + jnp.where(s, v2[part, :HD], zero)).astype(BF16)
            pv[(*cell, hi)] = jnp.where(s, zero, v2[part, HD:]).astype(BF16)
            pk[(*cell, lo)] = (k1[part] + jnp.where(s, k2[part, :HD], zero)).astype(BF16)
            pk[(*cell, hi)] = jnp.where(s, zero, k2[part, HD:]).astype(BF16)

        @pl.when((m == NZ - 1) & (c == half))
        def _():
            for j in range(2):
                part = slice(j * HALF, (j + 1) * HALF)
                pk[z, x, part] = (pk[z, x, part].astype(F32) + diag[2 * j, :, :HD]).astype(BF16)
                pv[z, x, part] = (pv[z, x, part].astype(F32) + diag[2 * j, :, HD:2 * HD]).astype(BF16)

        @pl.when(c == 1)
        def _():
            give(pv, m).start()

        @pl.when(c == 0)
        def _():
            give(pk, m).start()

    def add_into(dst, idx, *terms):
        total = dst[idx].astype(F32)
        for ref, i in terms:
            total = total + ref[i].astype(F32)
        dst[idx] = total.astype(BF16)

    def k_back(way, k, j):
        step = 1 if way == 0 else -1
        far = 2 if k == 4 else 1
        return remote(pk.at[zoff(step * k), xoff(j)], rr.at[way, k - 1, j],
                      rs.at[way, k - 1, j], rrsem.at[way, k - 1, j], at(zoff(step * far), x, 1))

    def k_across(j):
        return remote(pk.at[z, xoff(j)], xr.at[j], xs.at[j], xrsem.at[j], at(z, xoff(j), 1))

    def k_hop(m):
        give(pk, m).wait_recv()
        d = ORDER[NZ - 1 - m]
        k = abs(d)
        if k == 4:
            plan = [(w, j, ()) for i in range(2) for w, j in ((0, SETS[0][i]), (1, SETS[1][i]))]
        else:
            w = 0 if d > 0 else 1
            if k == 3:
                plan = [(w, j, ()) for j in ACROSS]
            elif k == 2:
                plan = [(w, j, (3, 4) if j in SETS[w] else (3,)) for j in SETS[1 - w] + SETS[w]]
            else:
                plan = [(w, j, (2,)) for j in SETS[1 - w] + SETS[w]]
        for w, j, has in plan:
            cell = (zoff(d), xoff(j))
            terms = [(sib, cell)]
            for q in has:
                k_back(w, q, j).wait_recv()
                terms.append((rr, (w, q - 1, j)))
            add_into(pk, cell, *terms)
            k_back(w, k, j).start()

    def k_last():
        give(pk, NZ - 1).wait_recv()
        for j in (2, 1, 3, 0):
            for w in range(2):
                k_back(w, 1, j).wait_recv()
            cell = (z, xoff(j))
            add_into(pk, cell, (sib, cell), (rr, (0, 0, j)), (rr, (1, 0, j)))
            if j:
                k_across(j).start()
        total = pk[z, x].astype(F32)
        for j in range(1, NX):
            k_across(j).wait_recv()
            total = total + xr[j].astype(F32)
        ysum[...] = total.astype(BF16)

    def v_back(d, m):
        return remote(pv.at[zoff(ORDER[NZ - 1 - m]), xoff(d)], cx.at[d, m], c1s.at[d, m],
                      c1r.at[d, m], at(z, xoff(d), 0))

    def v_z(m):
        d = ORDER[NZ - 1 - m]
        return remote(pv.at[zoff(d), x], zr.at[m], zs.at[m], zrsem.at[m], at(zoff(d), x, 0))

    def v_out(m):
        give(pv, m).wait_recv()
        for d in (2, 1, 3):
            cell = (zoff(ORDER[NZ - 1 - m]), xoff(d))
            add_into(pv, cell, (sib, cell))
            v_back(d, m).start()

    def v_in(m):
        cell = (zoff(ORDER[NZ - 1 - m]), x)
        terms = [(sib, cell)]
        for d in range(1, NX):
            v_back(d, m).wait_recv()
            terms.append((cx, (d, m)))
        add_into(pv, cell, *terms)
        if m < NZ - 1:
            v_z(m).start()

    def v_last():
        total = pv[z, x].astype(F32)
        for m in range(NZ - 1):
            v_z(m).wait_recv()
            total = total + zr[m].astype(F32)
        ysum[...] = total.astype(BF16)

    back = (
        {m: [(v_out, m - 2)] + ([(v_in, m - 6)] if m >= 6 else []) for m in range(2, NZ)},
        {2: [(k_hop, 0)], 3: [(k_hop, 1)], 4: [(k_hop, 2)]},
    )

    def drain_scatter():
        @pl.when(c == 1)
        def _():
            for w in range(2):
                for k in range(1, 5):
                    for j in range(NX):
                        if k < 4 or j in SETS[w]:
                            k_back(w, k, j).wait_send()
            for n in range(NZ):
                give(pv, n).wait_send()
            for j in range(1, NX):
                k_across(j).wait_send()

        @pl.when(c == 0)
        def _():
            for m in range(NZ):
                for d in range(1, NX):
                    v_back(d, m).wait_send()
                if m < NZ - 1:
                    v_z(m).wait_send()
                give(pk, m).wait_send()

    def scatter_step(m, _):
        gradient_row(m)
        run_plan(m, back)
        return 0

    lax.fori_loop(0, NZ, scatter_step, 0)

    @pl.when(c == 0)
    def _():
        v_out(6)
        v_out(7)

    for j, acc in enumerate((dq2[0:HD], dq2[HD:2 * HD] + dql[...])):
        g = (acc * INV_ROOT).T.astype(BF16)
        for i in range(2):
            for h in range(HEADS):
                at_row = i * ROWS + h * HALF
                dqst[i, j * HALF:(j + 1) * HALF, h * HD:(h + 1) * HD] = g[at_row:at_row + HALF]

    def dq_copy(i):
        if i == 0:
            return remote(dqst.at[0], dqr.at[0], dqs.at[0], dqsr.at[0], other(t, c))
        part = pl.ds((i - 1) * HALF, HALF)
        return remote(dqst.at[1, part], dqr.at[1, part], dqs.at[i], dqsr.at[i],
                      other(mates[i - 1], c))

    for i in range(3):
        dq_copy(i).start()

    @pl.when(c == 1)
    def _():
        for m in range(3, NZ - 1):
            k_hop(m)
        k_last()

    @pl.when(c == 0)
    def _():
        for m in range(2, NZ):
            v_in(m)
        v_last()

    def last(tt):
        return remote(ysum, yr.at[1 - c, t // 2], ys.at[tt], yrsem.at[1 - c, t // 2],
                      other(tt, half))

    for tt in range(NT):
        last(tt).start()

    drain_gather()
    drain_scatter()

    for i in range(3):
        dq_copy(i).wait()
    dq_out[0] = (dqr[0].astype(F32) + dqr[1].astype(F32)).astype(BF16)
    for kind, out in ((0, dk_out), (1, dv_out)):
        for i in range(2):
            landed(yrsem.at[kind, i])
        out[0] = (yr[kind, 0].astype(F32) + yr[kind, 1].astype(F32)).astype(BF16)
    for tt in range(NT):
        last(tt).wait_send()


def per_device(queries, keys, values, grad_out, span_order):
    vmem = pl.BlockSpec(memory_space=pltpu.VMEM)
    dma = pltpu.SemaphoreType.DMA

    def plane():
        return pltpu.VMEM((NZ, NX, 128, HD), BF16)

    scratch = [
        plane(),
        plane(),
        pltpu.VMEM((NZ, KEYS, SLOTS), F32),
        pltpu.VMEM((NZ, KEYS, SLOTS), F32),
        pltpu.VMEM((NZ, KEYS, SLOTS), F32),
        pltpu.VMEM((NZ, KEYS, SLOTS), F32),
        pltpu.VMEM((NZ, KEYS, 2 * HD), BF16),
        pltpu.VMEM((SLOTS, 2 * HD), BF16),
        pltpu.VMEM((SLOTS, 2 * HD), BF16),
        pltpu.VMEM((2, HALF, HEADS * HD), BF16),
        pltpu.VMEM((2, HALF, HEADS * HD), BF16),
        pltpu.VMEM((HD, SLOTS), F32),
        pltpu.VMEM((2 * HD, SLOTS), F32),
        pltpu.VMEM((2, 128, HEADS * HD), BF16),
        pltpu.VMEM((2, 128, HEADS * HD), BF16),
        pltpu.VMEM((8, SLOTS), F32),
        pltpu.VMEM((NZ + 1, 8, SLOTS), F32),
        pltpu.VMEM((4, HALF, SLOTS), F32),
        pltpu.VMEM((2, 8, SLOTS), F32),
        pltpu.VMEM((2, 8, SLOTS), F32),
        plane(),
        plane(),
        plane(),
        pltpu.VMEM((2, 4, NX, 128, HD), BF16),
        pltpu.VMEM((NX, NZ, 128, HD), BF16),
        pltpu.VMEM((NZ, 128, HD), BF16),
        pltpu.VMEM((NX, 128, HD), BF16),
        pltpu.VMEM((128, HD), BF16),
        pltpu.VMEM((2, 2, 128, HD), BF16),
        dma((NX,)), dma((NX,)), dma((NZ,)), dma((NZ,)),
        dma((2, 4, NX)), dma((2, 4, NX)), dma((NX, NZ)), dma((NX, NZ)),
        dma((NZ,)), dma((NZ,)),
        dma((2, 2)), dma((2, 2)), dma((2,)), dma((2,)),
        dma((NZ,)), dma((NZ,)),
        dma((2, 4, NX)), dma((2, 4, NX)),
        dma((NX, NZ)), dma((NX, NZ)),
        dma((NZ,)), dma((NZ,)), dma((NX,)), dma((NX,)),
        dma((NT,)), dma((2, 2)), dma((3,)), dma((3,)),
    ]
    return pl.pallas_call(
        kernel,
        out_shape=(
            jax.ShapeDtypeStruct(queries.shape, BF16),
            jax.ShapeDtypeStruct(keys.shape, BF16),
            jax.ShapeDtypeStruct(values.shape, BF16),
        ),
        in_specs=[vmem, vmem, vmem, vmem, pl.BlockSpec(memory_space=pltpu.SMEM)],
        out_specs=(vmem, vmem, vmem),
        scratch_shapes=scratch,
        compiler_params=pltpu.CompilerParams(
            collective_id=1, has_side_effects=True, vmem_limit_bytes=56 * 2**20
        ),
        name="attention_backward",
    )(queries, keys, values, grad_out, jnp.swapaxes(span_order, 1, 2))


def solution(mesh):
    return jax.shard_map(
        per_device,
        mesh=mesh,
        in_specs=(
            P("pipe", "ctx", "tp"),
            P("pipe", "ctx", None),
            P("pipe", "ctx", None),
            P("pipe", "ctx", "tp"),
            P("pipe", None, None),
        ),
        out_specs=(P("pipe", "ctx", "tp"), P("pipe", "ctx", None), P("pipe", "ctx", None)),
        check_vma=False,
    )
```

time: 82.5 us -> 69.2 us (0.84)
  Pallas kernels: 77.2 us -> 65.4 us
  local copies, waits for them, and re-layouts: 4.34 us -> 2.96 us
    pallas_call x1, Pallas kernels: 77.2 us -> 65.4 us  [per_device(): pl.pallas_call(kernel, out_shape=(jax.ShapeDtypeStruct(queries.shape, BF1...]
    unnamed x8 -> x7, local copies, waits for them, and re-layouts: 4.34 us -> 2.96 us
where the time goes in v3:
time: 69.2 us; the launch traced here: 69 us
  Pallas kernels  65.4 us (95%)
  local copies, waits for them, and re-layouts  2.96 us (4%)
    pallas_call x1, Pallas kernels, per_device(): pl.pallas_call(kernel, out_shape=(jax.ShapeDtypeStruct(queries.shape, BF1...  65.4 us
    unnamed x7, local copies, waits for them, and re-layouts  2.96 us

profile of v3, /device:TPU:1, one launch (start us, length us, event | category | flops | bytes accessed | tf_op | source)
XLA Modules:
  0.0 69.0 jit_solution(16391635488864359820)
XLA Ops:
  0.6 65.4 %attention_backward.1 = (bf16[1,128,512]{2,1,0:T(8,128)(2,1)}, bf16[1,128,128]{2,1,0:T(8,128)(2,1)}, bf16[1,128,128]{2,1,0:T(8,128)(2,1)}) custom-call(bf16[1,128,512]{2,1,0:T(8,128)(2,1)} %q_ref.1, bf16[1,128,128]{2,1,0:T(8,128)(2,1)} %k_ref.1, bf16[1,128,128]{2,1,0:T(8,128)(2,1)} %v_ref.1, bf16[1,128,512]{2,1,0:T(8,128)(2,1)} %g_ref.1, s32[1,2,64]{2,1,0:T(2,128)} %bitcast.1), custom_call_target="tpu_custom_call" | custom-call | tf_op jit(solution)/shard_map/attention_backward/pallas_call | solution.py:717
  66.0 0.0 copy-start.1
  66.0 1.6 %copy.11 = bf16[1,128,512]{2,1,0:T(8,128)(2,1)} copy(bf16[1,128,512]{2,1,0:T(8,128)(2,1)} %get-tuple-element.6) | data formatting | bytes 262144
  67.6 0.0 copy-done.1
  67.6 0.0 copy-start
  67.6 0.6 copy.12
  68.2 0.2 copy-done
  68.4 0.6 copy.13
Async XLA Ops:
  66.0 1.6 %copy-start.1 = (bf16[1,128,128]{2,1,0:T(8,128)(2,1)S(1)}, bf16[1,128,128]{2,1,0:T(8,128)(2,1)}, u32[]{:S(2)}) copy-start(bf16[1,128,128]{2,1,0:T(8,128)(2,1)} %get-tuple-element.7) | copy-start | bytes 98308
  67.6 0.8 %copy-start = (bf16[1,128,128]{2,1,0:T(8,128)(2,1)S(1)}, bf16[1,128,128]{2,1,0:T(8,128)(2,1)}, u32[]{:S(2)}) copy-start(bf16[1,128,128]{2,1,0:T(8,128)(2,1)} %get-tuple-element.8) | copy-start | bytes 98308

commit v4 on v3

--- a/solution.py
+++ b/solution.py
@@ -50,13 +50,13 @@
 
 
 def kernel(
-    q_ref, k_ref, v_ref, g_ref, span_ref,
+    q_hbm, k_hbm, v_hbm, g_hbm, span_ref,
     dq_out, dk_out, dv_out,
-    kbuf, vbuf, s1, s2, dp1, dp2, kselbuf, qq, oo, pq, pg, dql, dq2, dqst, dqr,
+    q_ref, k_ref, v_ref, g_ref, kbuf, vbuf, s1, s2, dp1, dp2, kselbuf, qq, oo, pq, pg, dql, dq2, dqst, dqr,
     state, tops, diag, sums_out, sums_in,
     pk, pv, sib, rr, cx, zr, xr, ysum, yr,
-    p1ks, p1kr, p1vs, p1vr, zks, zkr, x1s, x1r, d2ds, d2dr,
-    pqs, pqr, sums_s, sums_r, sibs, sibr, rs, rrsem, c1s, c1r, zs, zrsem, xs, xrsem, ys, yrsem, dqs, dqsr,
+    insem, sent, p1kr, p1vr, zkr, x1r, d2dr, pqr, sums_r, sibr, rrsem, c1r, zrsem, xrsem,
+    yrsem, dqsr,
 ):
     pipe = lax.axis_index("pipe")
     me = lax.axis_index("ctx")
@@ -92,6 +92,13 @@
             src_ref=src, dst_ref=dst, send_sem=ssem, recv_sem=rsem,
             device_id=dev, device_id_type=MESH,
         )
+
+    def take(i):
+        src = (q_hbm, g_hbm, k_hbm, v_hbm)[i]
+        return pltpu.make_async_copy(src, (q_ref, g_ref, k_ref, v_ref)[i], insem.at[0])
+
+    for i in range(4):
+        take(i).start()
 
     barrier = pltpu.get_barrier_semaphore()
     count = 0
@@ -120,9 +127,6 @@
             dst[base + h * HALF:base + (h + 1) * HALF, j * HD:(j + 1) * HD] = src[
                 lo:lo + HALF, h * HD:(h + 1) * HD]
 
-    for j in range(2):
-        lay_rows(qq, 0, q_ref.at[0], j * HALF, j)
-        lay_rows(oo, 0, g_ref.at[0], j * HALF, j)
     low = jnp.full((1, SLOTS), NEG, F32)
     state[...] = jnp.zeros_like(state)
     sums_out[...] = jnp.zeros_like(sums_out)
@@ -135,37 +139,41 @@
     pl.semaphore_wait(barrier, count)
 
     def swap_rows(j, kind):
-        src = (q_ref, g_ref)[kind].at[0, pl.ds(j * HALF, HALF)]
+        src = (q_hbm, g_hbm)[kind].at[0, pl.ds(j * HALF, HALF)]
         dst = (pq, pg)[kind].at[j]
-        return remote(src, dst, pqs.at[j, kind], pqr.at[j, kind], mate(j))
+        return remote(src, dst, sent.at[4], pqr.at[0], mate(j))
 
     for kind in range(2):
         for j in range(2):
             swap_rows(j, kind).start()
 
     def first_k(d):
-        return remote(k_ref.at[0], kbuf.at[z, x], p1ks.at[d], p1kr.at[d], at(z, xoff(d), 1))
+        return remote(k_hbm.at[0], kbuf.at[z, x], sent.at[0], p1kr.at[d], at(z, xoff(d), 1))
 
     def first_v(d):
-        return remote(v_ref.at[0], vbuf.at[z, x], p1vs.at[d], p1vr.at[d], at(zoff(d), x, 0))
+        return remote(v_hbm.at[0], vbuf.at[z, x], sent.at[0], p1vr.at[d], at(zoff(d), x, 0))
+
+    def k_slot(way, k, j):
+        return {1: way, 2: 5 + way * 4 + j, 3: 2 + way, 4: 4}[k]
 
     def k_send(way, k, j):
         step = 1 if way == 0 else -1
-        back, far = (2, 2) if k == 4 else (k - 1, 1)
+        back, far = ((0, 1), (0, 2), (2, 1), (2, 2))[k - 1]
         ref = kbuf.at[zoff(-step * back), xoff(j)]
-        return remote(ref, ref, zks.at[way, k - 1, j], zkr.at[way, k - 1, j],
+        return remote(ref, ref, sent.at[1], zkr.at[k_slot(way, k, j)],
                       at(zoff(step * far), x, 1))
 
     def v_x(d, n):
         ref = vbuf.at[zoff(ORDER[n]), x]
-        return remote(ref, ref, x1s.at[d, n], x1r.at[d, n], at(z, xoff(d), 0))
+        return remote(ref, ref, sent.at[2], x1r.at[n], at(z, xoff(d), 0))
 
     def hand_over(buf, n):
         ref = buf.at[row_of(n)]
-        return remote(ref, ref, d2ds.at[n], d2dr.at[n], sibling)
-
-    def landed(sem):
-        pltpu.make_async_copy(kbuf.at[0, 0], kbuf.at[0, 0], sem).wait()
+        return remote(ref, ref, sent.at[3], d2dr.at[n], sibling)
+
+    def landed(sem, n=1):
+        ref = cx.at[pl.ds(0, n)]
+        pltpu.make_async_copy(ref, ref, sem).wait()
 
     def gather_k(n):
         d = ORDER[n]
@@ -180,21 +188,17 @@
                     def _():
                         landed(p1kr.at[0])
                 for w in range(2):
+                    k_send(w, 2, j).start()
                     k_send(w, 1, j).start()
-        elif k < 4:
+        elif k == 2:
             w = 1 if d > 0 else 0
             for j in ACROSS:
-                k_send(w, k, j).wait_recv()
-                if k == 1:
-                    k_send(w, 2, j).start()
-                if k == 2:
-                    if j in SETS[w]:
-                        k_send(w, 4, j).start()
-                    k_send(w, 3, j).start()
+                landed(zkr.at[k_slot(w, 2, j)])
+                if j in SETS[w]:
+                    k_send(w, 4, j).start()
+                k_send(w, 3, j).start()
         else:
-            for w in range(2):
-                for j in SETS[w]:
-                    k_send(w, 4, j).wait_recv()
+            landed(zkr.at[k_slot(1 if d > 0 else 0, k, 0)], NX)
         hand_over(kbuf, n).start()
 
     def v_stage1(n):
@@ -209,9 +213,11 @@
             v_x(dx, n).start()
 
     def v_stage2(n):
-        for dx in range(1, NX):
-            v_x(dx, n).wait_recv()
+        landed(x1r.at[n], NX - 1)
         hand_over(vbuf, n).start()
+
+    def keep(src, buf):
+        return pltpu.make_async_copy(src.at[0], buf.at[z, x], insem.at[1])
 
     @pl.when(c == half)
     def _():
@@ -221,53 +227,39 @@
         @pl.when(c == 0)
         def _():
             first_k(0).start()
-            vbuf[z, x] = v_ref[0]
+            keep(v_hbm, vbuf).start()
 
         @pl.when(c == 1)
         def _():
             first_v(0).start()
-            kbuf[z, x] = k_ref[0]
+            keep(k_hbm, kbuf).start()
 
         for d in (1, 7, 2, 6, 3, 5, 4):
             first_v(d).start()
 
+        keep(k_hbm, kbuf).wait()
+
+    landed(insem.at[0], 10)
+    for j in range(2):
+        lay_rows(qq, 0, q_ref.at[0], j * HALF, j)
+        lay_rows(oo, 0, g_ref.at[0], j * HALF, j)
+
     def drain_gather():
         @pl.when(c == 1)
         def _():
-            for w in range(2):
-                for k in range(1, 5):
-                    for j in range(NX):
-                        if k < 4 or j in SETS[w]:
-                            k_send(w, k, j).wait_send()
-            for n in range(NZ):
-                hand_over(kbuf, n).wait_send()
+            landed(sent.at[1], 28)
 
         @pl.when(c == 0)
         def _():
-            for n in range(NZ):
-                for dx in range(1, NX):
-                    v_x(dx, n).wait_send()
-                hand_over(vbuf, n).wait_send()
+            landed(sent.at[2], 24)
 
         @pl.when(c == half)
         def _():
-            for d in range(1, NX):
-                first_k(d).wait_send()
-            for d in range(1, NZ):
-                first_v(d).wait_send()
-
-            @pl.when(c == 0)
-            def _():
-                first_k(0).wait_send()
-
-            @pl.when(c == 1)
-            def _():
-                first_v(0).wait_send()
-
-        for j in range(2):
-            for kind in range(2):
-                swap_rows(j, kind).wait_send()
-            swap_sums(j).wait_send()
+            landed(sent.at[0], 11)
+
+        landed(sent.at[3], 32)
+        landed(sent.at[4], 8)
+        landed(sent.at[5], 1)
 
     my_block = span_ref[0, 0, me]
 
@@ -362,20 +354,21 @@
             tops[NZ, j:j + 1] = top
 
     def swap_sums(j):
-        return remote(sums_out.at[j], sums_in.at[j], sums_s.at[j], sums_r.at[j], mate(j))
-
-    LAG = 5
+        return remote(sums_out.at[j], sums_in.at[j], sent.at[5], sums_r.at[0], mate(j))
+
+    LAG = 2
     plans = (
         {
             0: [(v_stage1, n) for n in range(5)],
-            1: [(v_stage1, 5), (v_stage1, 6), (v_stage1, 7), (v_stage2, 0), (v_stage2, 1)],
-            2: [(v_stage2, 2), (v_stage2, 3)],
-            3: [(v_stage2, 4)],
-            4: [(v_stage2, 5)],
-            5: [(v_stage2, 6)],
-            6: [(v_stage2, 7)],
+            1: [(v_stage1, 5), (v_stage1, 6), (v_stage1, 7)] + [(v_stage2, n) for n in range(3)],
+            3: [(v_stage2, 3), (v_stage2, 4)],
+            5: [(v_stage2, 5), (v_stage2, 6), (v_stage2, 7)],
         },
-        {n: [(gather_k, n)] for n in range(NZ)},
+        {
+            0: [(gather_k, 0), (gather_k, 3), (gather_k, 4)],
+            1: [(gather_k, 1), (gather_k, 2)],
+            6: [(gather_k, 5), (gather_k, 6), (gather_k, 7)],
+        },
     )
 
     def run_plan(i, plans):
@@ -391,9 +384,9 @@
 
         @pl.when(i == LAG)
         def _():
+            landed(pqr.at[0], 8)
             for kind in range(2):
                 for j in range(2):
-                    swap_rows(j, kind).wait_recv()
                     lay_rows((qq, oo)[kind], ROWS, (pq, pg)[kind].at[j], 0, j)
 
             @pl.when(c == half)
@@ -412,8 +405,8 @@
         for i in range(3):
             sums_out[j, i:i + 1] = state[2 * i + j:2 * i + j + 1]
         swap_sums(j).start()
+    landed(sums_r.at[0])
     for j in range(2):
-        swap_sums(j).wait_recv()
         m, l, d = (state[2 * i + j:2 * i + j + 1] for i in range(3))
         m2, l2, d2 = (
             jnp.concatenate([sums_in[j, i:i + 1, ROWS:], sums_in[j, i:i + 1, :ROWS]], axis=1)
@@ -440,7 +433,7 @@
 
     def give(buf, m):
         b = row_of(NZ - 1 - m)
-        return remote(buf.at[b], sib.at[b], sibs.at[m], sibr.at[m], sibling)
+        return remote(buf.at[b], sib.at[b], sent.at[6], sibr.at[m], sibling)
 
     def gradient_row(m):
         b = row_of(NZ - 1 - m)
@@ -501,12 +494,12 @@
 
     def k_back(way, k, j):
         step = 1 if way == 0 else -1
-        far = 2 if k == 4 else 1
+        far = (1, 2, 1, 2)[k - 1]
         return remote(pk.at[zoff(step * k), xoff(j)], rr.at[way, k - 1, j],
-                      rs.at[way, k - 1, j], rrsem.at[way, k - 1, j], at(zoff(step * far), x, 1))
+                      sent.at[7], rrsem.at[8 + j if k < 3 else way * 4 + j], at(zoff(step * far), x, 1))
 
     def k_across(j):
-        return remote(pk.at[z, xoff(j)], xr.at[j], xs.at[j], xrsem.at[j], at(z, xoff(j), 1))
+        return remote(pk.at[z, xoff(j)], xr.at[j], sent.at[10], xrsem.at[0], at(z, xoff(j), 1))
 
     def k_hop(m):
         give(pk, m).wait_recv()
@@ -521,12 +514,13 @@
             elif k == 2:
                 plan = [(w, j, (3, 4) if j in SETS[w] else (3,)) for j in SETS[1 - w] + SETS[w]]
             else:
-                plan = [(w, j, (2,)) for j in SETS[1 - w] + SETS[w]]
+                plan = [(w, j, ()) for j in ACROSS]
         for w, j, has in plan:
             cell = (zoff(d), xoff(j))
             terms = [(sib, cell)]
+            if has:
+                landed(rrsem.at[w * 4 + j], len(has))
             for q in has:
-                k_back(w, q, j).wait_recv()
                 terms.append((rr, (w, q - 1, j)))
             add_into(pk, cell, *terms)
             k_back(w, k, j).start()
@@ -534,25 +528,28 @@
     def k_last():
         give(pk, NZ - 1).wait_recv()
         for j in (2, 1, 3, 0):
+            landed(rrsem.at[8 + j], 4)
+            cell = (z, xoff(j))
+            terms = [(sib, cell)]
             for w in range(2):
-                k_back(w, 1, j).wait_recv()
-            cell = (z, xoff(j))
-            add_into(pk, cell, (sib, cell), (rr, (0, 0, j)), (rr, (1, 0, j)))
+                for k in (1, 2):
+                    terms.append((rr, (w, k - 1, j)))
+            add_into(pk, cell, *terms)
             if j:
                 k_across(j).start()
         total = pk[z, x].astype(F32)
+        landed(xrsem.at[0], NX - 1)
         for j in range(1, NX):
-            k_across(j).wait_recv()
             total = total + xr[j].astype(F32)
         ysum[...] = total.astype(BF16)
 
     def v_back(d, m):
-        return remote(pv.at[zoff(ORDER[NZ - 1 - m]), xoff(d)], cx.at[d, m], c1s.at[d, m],
-                      c1r.at[d, m], at(z, xoff(d), 0))
+        return remote(pv.at[zoff(ORDER[NZ - 1 - m]), xoff(d)], cx.at[d * NZ + m], sent.at[8],
+                      c1r.at[m], at(z, xoff(d), 0))
 
     def v_z(m):
         d = ORDER[NZ - 1 - m]
-        return remote(pv.at[zoff(d), x], zr.at[m], zs.at[m], zrsem.at[m], at(zoff(d), x, 0))
+        return remote(pv.at[zoff(d), x], zr.at[m], sent.at[9], zrsem.at[0], at(zoff(d), x, 0))
 
     def v_out(m):
         give(pv, m).wait_recv()
@@ -564,17 +561,17 @@
     def v_in(m):
         cell = (zoff(ORDER[NZ - 1 - m]), x)
         terms = [(sib, cell)]
+        landed(c1r.at[m], NX - 1)
         for d in range(1, NX):
-            v_back(d, m).wait_recv()
-            terms.append((cx, (d, m)))
+            terms.append((cx, d * NZ + m))
         add_into(pv, cell, *terms)
         if m < NZ - 1:
             v_z(m).start()
 
     def v_last():
         total = pv[z, x].astype(F32)
+        landed(zrsem.at[0], NZ - 1)
         for m in range(NZ - 1):
-            v_z(m).wait_recv()
             total = total + zr[m].astype(F32)
         ysum[...] = total.astype(BF16)
 
@@ -586,24 +583,15 @@
     def drain_scatter():
         @pl.when(c == 1)
         def _():
-            for w in range(2):
-                for k in range(1, 5):
-                    for j in range(NX):
-                        if k < 4 or j in SETS[w]:
-                            k_back(w, k, j).wait_send()
-            for n in range(NZ):
-                give(pv, n).wait_send()
-            for j in range(1, NX):
-                k_across(j).wait_send()
+            landed(sent.at[7], 28)
+            landed(sent.at[10], 3)
 
         @pl.when(c == 0)
         def _():
-            for m in range(NZ):
-                for d in range(1, NX):
-                    v_back(d, m).wait_send()
-                if m < NZ - 1:
-                    v_z(m).wait_send()
-                give(pk, m).wait_send()
+            landed(sent.at[8], 24)
+            landed(sent.at[9], 7)
+
+        landed(sent.at[6], 32)
 
     def scatter_step(m, _):
         gradient_row(m)
@@ -616,6 +604,13 @@
     def _():
         v_out(6)
         v_out(7)
+        for m in range(2, 5):
+            v_in(m)
+
+    @pl.when(c == 1)
+    def _():
+        for m in range(3, NZ - 1):
+            k_hop(m)
 
     for j, acc in enumerate((dq2[0:HD], dq2[HD:2 * HD] + dql[...])):
         g = (acc * INV_ROOT).T.astype(BF16)
@@ -626,9 +621,9 @@
 
     def dq_copy(i):
         if i == 0:
-            return remote(dqst.at[0], dqr.at[0], dqs.at[0], dqsr.at[0], other(t, c))
+            return remote(dqst.at[0], dqr.at[0], sent.at[12], dqsr.at[0], other(t, c))
         part = pl.ds((i - 1) * HALF, HALF)
-        return remote(dqst.at[1, part], dqr.at[1, part], dqs.at[i], dqsr.at[i],
+        return remote(dqst.at[1, part], dqr.at[1, part], sent.at[12], dqsr.at[0],
                       other(mates[i - 1], c))
 
     for i in range(3):
@@ -636,18 +631,16 @@
 
     @pl.when(c == 1)
     def _():
-        for m in range(3, NZ - 1):
-            k_hop(m)
         k_last()
 
     @pl.when(c == 0)
     def _():
-        for m in range(2, NZ):
+        for m in range(5, NZ):
             v_in(m)
         v_last()
 
     def last(tt):
-        return remote(ysum, yr.at[1 - c, t // 2], ys.at[tt], yrsem.at[1 - c, t // 2],
+        return remote(ysum, yr.at[1 - c, t // 2], sent.at[11], yrsem.at[0],
                       other(tt, half))
 
     for tt in range(NT):
@@ -656,25 +649,28 @@
     drain_gather()
     drain_scatter()
 
-    for i in range(3):
-        dq_copy(i).wait()
+    landed(dqsr.at[0], 8)
     dq_out[0] = (dqr[0].astype(F32) + dqr[1].astype(F32)).astype(BF16)
+    landed(yrsem.at[0], 4)
     for kind, out in ((0, dk_out), (1, dv_out)):
-        for i in range(2):
-            landed(yrsem.at[kind, i])
         out[0] = (yr[kind, 0].astype(F32) + yr[kind, 1].astype(F32)).astype(BF16)
-    for tt in range(NT):
-        last(tt).wait_send()
+    landed(sent.at[11], 4)
+    landed(sent.at[12], 8)
 
 
 def per_device(queries, keys, values, grad_out, span_order):
     vmem = pl.BlockSpec(memory_space=pltpu.VMEM)
+    hbm = pl.BlockSpec(memory_space=pl.ANY)
     dma = pltpu.SemaphoreType.DMA
 
     def plane():
         return pltpu.VMEM((NZ, NX, 128, HD), BF16)
 
     scratch = [
+        pltpu.VMEM(queries.shape, BF16),
+        pltpu.VMEM(keys.shape, BF16),
+        pltpu.VMEM(values.shape, BF16),
+        pltpu.VMEM(grad_out.shape, BF16),
         plane(),
         plane(),
         pltpu.VMEM((NZ, KEYS, SLOTS), F32),
@@ -699,20 +695,16 @@
         plane(),
         plane(),
         pltpu.VMEM((2, 4, NX, 128, HD), BF16),
-        pltpu.VMEM((NX, NZ, 128, HD), BF16),
+        pltpu.VMEM((NX * NZ, 128, HD), BF16),
         pltpu.VMEM((NZ, 128, HD), BF16),
         pltpu.VMEM((NX, 128, HD), BF16),
         pltpu.VMEM((128, HD), BF16),
         pltpu.VMEM((2, 2, 128, HD), BF16),
-        dma((NX,)), dma((NX,)), dma((NZ,)), dma((NZ,)),
-        dma((2, 4, NX)), dma((2, 4, NX)), dma((NX, NZ)), dma((NX, NZ)),
-        dma((NZ,)), dma((NZ,)),
-        dma((2, 2)), dma((2, 2)), dma((2,)), dma((2,)),
-        dma((NZ,)), dma((NZ,)),
-        dma((2, 4, NX)), dma((2, 4, NX)),
-        dma((NX, NZ)), dma((NX, NZ)),
-        dma((NZ,)), dma((NZ,)), dma((NX,)), dma((NX,)),
-        dma((NT,)), dma((2, 2)), dma((3,)), dma((3,)),
+        dma((2,)), dma((13,)),
+        dma((NX,)), dma((NZ,)), dma((13,)), dma((NZ,)), dma((NZ,)),
+        dma((1,)), dma((1,)),
+        dma((NZ,)), dma((12,)), dma((NZ,)), dma((1,)), dma((1,)),
+        dma((1,)), dma((1,)),
     ]
     return pl.pallas_call(
         kernel,
@@ -721,7 +713,7 @@
             jax.ShapeDtypeStruct(keys.shape, BF16),
             jax.ShapeDtypeStruct(values.shape, BF16),
         ),
-        in_specs=[vmem, vmem, vmem, vmem, pl.BlockSpec(memory_space=pltpu.SMEM)],
+        in_specs=[hbm, hbm, hbm, hbm, pl.BlockSpec(memory_space=pltpu.SMEM)],
         out_specs=(vmem, vmem, vmem),
         scratch_shapes=scratch,
         compiler_params=pltpu.CompilerParams(

time: 69.2 us -> 65.2 us (0.942)
  Pallas kernels: 65.4 us -> 61.3 us
    pallas_call x1, Pallas kernels: 65.4 us -> 61.3 us  [per_device(): pl.pallas_call(kernel, out_shape=(jax.ShapeDtypeStruct(queries.shape, BF1...]
where the time goes in v4:
time: 65.2 us; the launch traced here: 64.9 us
  Pallas kernels  61.3 us (94%)
  local copies, waits for them, and re-layouts  2.96 us (5%)
    pallas_call x1, Pallas kernels, per_device(): pl.pallas_call(kernel, out_shape=(jax.ShapeDtypeStruct(queries.shape, BF1...  61.3 us
    unnamed x7, local copies, waits for them, and re-layouts  2.96 us

profile of v4, /device:TPU:1, one launch (start us, length us, event | category | flops | bytes accessed | tf_op | source)
XLA Modules:
  0.0 64.9 jit_solution(22416780755856061)
XLA Ops:
  0.6 61.3 %attention_backward.1 = (bf16[1,128,512]{2,1,0:T(8,128)(2,1)}, bf16[1,128,128]{2,1,0:T(8,128)(2,1)}, bf16[1,128,128]{2,1,0:T(8,128)(2,1)}) custom-call(bf16[1,128,512]{2,1,0:T(8,128)(2,1)} %q_hbm.1, bf16[1,128,128]{2,1,0:T(8,128)(2,1)} %k_hbm.1, bf16[1,128,128]{2,1,0:T(8,128)(2,1)} %v_hbm.1, bf16[1,128,512]{2,1,0:T(8,128)(2,1)} %g_hbm.1, s32[1,2,64]{2,1,0:T(2,128)} %bitcast.1), custom_call_target="tpu_custom_call" | custom-call | tf_op jit(solution)/shard_map/attention_backward/pallas_call | solution.py:709
  61.9 0.0 copy-start.1
  61.9 1.6 %copy.11 = bf16[1,128,512]{2,1,0:T(8,128)(2,1)} copy(bf16[1,128,512]{2,1,0:T(8,128)(2,1)} %get-tuple-element.6) | data formatting | bytes 262144
  63.5 0.0 copy-done.1
  63.5 0.0 copy-start
  63.5 0.6 copy.12
  64.1 0.2 copy-done
  64.3 0.6 copy.13
Async XLA Ops:
  61.9 1.6 %copy-start.1 = (bf16[1,128,128]{2,1,0:T(8,128)(2,1)S(1)}, bf16[1,128,128]{2,1,0:T(8,128)(2,1)}, u32[]{:S(2)}) copy-start(bf16[1,128,128]{2,1,0:T(8,128)(2,1)} %get-tuple-element.7) | copy-start | bytes 98308
  63.5 0.8 %copy-start = (bf16[1,128,128]{2,1,0:T(8,128)(2,1)S(1)}, bf16[1,128,128]{2,1,0:T(8,128)(2,1)}, u32[]{:S(2)}) copy-start(bf16[1,128,128]{2,1,0:T(8,128)(2,1)} %get-tuple-element.8) | copy-start | bytes 98308

commit v5 on v4

--- a/solution.py
+++ b/solution.py
@@ -20,11 +20,17 @@
 ROWS = HEADS * HALF
 SLOTS = 2 * ROWS
 KEYS = NX * HALF
+BLOCK = 256
+SPLIT = 112
+REST = BLOCK - SPLIT
+FIRST = pl.ds(0, SPLIT)
+SECOND = pl.ds(SPLIT, REST)
 INV_ROOT = HD ** (-0.5)
 LOG2E = 1.4426950408889634
 NEG = -1e30
 POS = 1e30
 ORDER = (0, 1, -1, 2, -2, 3, -3, 4)
+BACK = (4, -3, 3, -1, 1, -2, 2, 0)
 ACROSS = (0, 1, 3, 2)
 SETS = ((0, 1), (3, 2))
 
@@ -52,9 +58,9 @@
 def kernel(
     q_hbm, k_hbm, v_hbm, g_hbm, span_ref,
     dq_out, dk_out, dv_out,
-    q_ref, k_ref, v_ref, g_ref, kbuf, vbuf, s1, s2, dp1, dp2, kselbuf, qq, oo, pq, pg, dql, dq2, dqst, dqr,
+    q_ref, k_ref, v_ref, g_ref, kv, s1, s2, dp1, dp2, kselbuf, qq, oo, pq, pg, dql, dq2, dqst, dqr,
     state, tops, diag, sums_out, sums_in,
-    pk, pv, sib, rr, cx, zr, xr, ysum, yr,
+    pkv, sib, rr, cx, zr, xr, ysum, yr,
     insem, sent, p1kr, p1vr, zkr, x1r, d2dr, pqr, sums_r, sibr, rrsem, c1r, zrsem, xrsem,
     yrsem, dqsr,
 ):
@@ -81,6 +87,12 @@
 
     def mate(j):
         return (pipe, me, mates[j])
+
+    def back_row(m):
+        d = 0
+        for i, far in enumerate(BACK):
+            d = jnp.where(m == i, far, d)
+        return zoff(d)
 
     def other(tt, cc):
         return (1 - pipe, (z * NX + x) * 2 + cc, tt)
@@ -148,10 +160,15 @@
             swap_rows(j, kind).start()
 
     def first_k(d):
-        return remote(k_hbm.at[0], kbuf.at[z, x], sent.at[0], p1kr.at[d], at(z, xoff(d), 1))
+        return remote(k_hbm.at[0, FIRST], kv.at[z, x, FIRST], sent.at[0], p1kr.at[d],
+                      at(z, xoff(d), 1))
 
     def first_v(d):
-        return remote(v_hbm.at[0], vbuf.at[z, x], sent.at[0], p1vr.at[d], at(zoff(d), x, 0))
+        there = at(zoff(d), x, 0)
+        keys = remote(k_hbm.at[0, pl.ds(SPLIT, 128 - SPLIT)], kv.at[z, x, pl.ds(SPLIT, 128 - SPLIT)],
+                      sent.at[0], p1vr.at[d], there)
+        values = remote(v_hbm.at[0], kv.at[z, x, pl.ds(128, 128)], sent.at[0], p1vr.at[d], there)
+        return keys, values
 
     def k_slot(way, k, j):
         return {1: way, 2: 5 + way * 4 + j, 3: 2 + way, 4: 4}[k]
@@ -159,20 +176,20 @@
     def k_send(way, k, j):
         step = 1 if way == 0 else -1
         back, far = ((0, 1), (0, 2), (2, 1), (2, 2))[k - 1]
-        ref = kbuf.at[zoff(-step * back), xoff(j)]
+        ref = kv.at[zoff(-step * back), xoff(j), FIRST]
         return remote(ref, ref, sent.at[1], zkr.at[k_slot(way, k, j)],
                       at(zoff(step * far), x, 1))
 
     def v_x(d, n):
-        ref = vbuf.at[zoff(ORDER[n]), x]
+        ref = kv.at[zoff(ORDER[n]), x, SECOND]
         return remote(ref, ref, sent.at[2], x1r.at[n], at(z, xoff(d), 0))
 
-    def hand_over(buf, n):
-        ref = buf.at[row_of(n)]
+    def hand_over(part, n):
+        ref = kv.at[row_of(n), :, part]
         return remote(ref, ref, sent.at[3], d2dr.at[n], sibling)
 
-    def landed(sem, n=1):
-        ref = cx.at[pl.ds(0, n)]
+    def landed(sem, rows):
+        ref = cx.at[pl.ds(0, rows)]
         pltpu.make_async_copy(ref, ref, sem).wait()
 
     def gather_k(n):
@@ -182,42 +199,47 @@
             for j in ACROSS:
                 src = (NX - j) % NX
                 if src:
-                    landed(p1kr.at[src])
+                    landed(p1kr.at[src], SPLIT)
                 else:
                     @pl.when(half == 0)
                     def _():
-                        landed(p1kr.at[0])
+                        landed(p1kr.at[0], SPLIT)
                 for w in range(2):
                     k_send(w, 2, j).start()
                     k_send(w, 1, j).start()
         elif k == 2:
             w = 1 if d > 0 else 0
             for j in ACROSS:
-                landed(zkr.at[k_slot(w, 2, j)])
+                landed(zkr.at[k_slot(w, 2, j)], SPLIT)
                 if j in SETS[w]:
                     k_send(w, 4, j).start()
                 k_send(w, 3, j).start()
         else:
-            landed(zkr.at[k_slot(1 if d > 0 else 0, k, 0)], NX)
-        hand_over(kbuf, n).start()
+            landed(zkr.at[k_slot(1 if d > 0 else 0, k, 0)], NX * SPLIT)
+        hand_over(FIRST, n).start()
 
     def v_stage1(n):
         d = ORDER[n]
         if d:
-            landed(p1vr.at[-d % NZ])
+            landed(p1vr.at[-d % NZ], REST)
         else:
             @pl.when(half == 1)
             def _():
-                landed(p1vr.at[0])
+                landed(p1vr.at[0], REST)
         for dx in (1, 3, 2):
             v_x(dx, n).start()
 
     def v_stage2(n):
-        landed(x1r.at[n], NX - 1)
-        hand_over(vbuf, n).start()
-
-    def keep(src, buf):
-        return pltpu.make_async_copy(src.at[0], buf.at[z, x], insem.at[1])
+        landed(x1r.at[n], (NX - 1) * REST)
+        hand_over(SECOND, n).start()
+
+    def keep(i):
+        part = pl.ds(0, SPLIT) if i == 0 else pl.ds(SPLIT, 128 - SPLIT)
+        if i == 2:
+            src, dst = v_hbm.at[0], kv.at[z, x, pl.ds(128, 128)]
+        else:
+            src, dst = k_hbm.at[0, part], kv.at[z, x, part]
+        return pltpu.make_async_copy(src, dst, insem.at[1])
 
     @pl.when(c == half)
     def _():
@@ -227,19 +249,28 @@
         @pl.when(c == 0)
         def _():
             first_k(0).start()
-            keep(v_hbm, vbuf).start()
+            keep(1).start()
+            keep(2).start()
 
         @pl.when(c == 1)
         def _():
-            first_v(0).start()
-            keep(k_hbm, kbuf).start()
+            for cp in first_v(0):
+                cp.start()
+            keep(0).start()
 
         for d in (1, 7, 2, 6, 3, 5, 4):
-            first_v(d).start()
-
-        keep(k_hbm, kbuf).wait()
-
-    landed(insem.at[0], 10)
+            for cp in first_v(d):
+                cp.start()
+
+        @pl.when(c == 0)
+        def _():
+            landed(insem.at[1], REST)
+
+        @pl.when(c == 1)
+        def _():
+            landed(insem.at[1], SPLIT)
+
+    landed(insem.at[0], 10 * 128)
     for j in range(2):
         lay_rows(qq, 0, q_ref.at[0], j * HALF, j)
         lay_rows(oo, 0, g_ref.at[0], j * HALF, j)
@@ -247,19 +278,24 @@
     def drain_gather():
         @pl.when(c == 1)
         def _():
-            landed(sent.at[1], 28)
+            landed(sent.at[1], 28 * SPLIT)
+            landed(sent.at[3], NZ * NX * SPLIT)
 
         @pl.when(c == 0)
         def _():
-            landed(sent.at[2], 24)
-
-        @pl.when(c == half)
-        def _():
-            landed(sent.at[0], 11)
-
-        landed(sent.at[3], 32)
-        landed(sent.at[4], 8)
-        landed(sent.at[5], 1)
+            landed(sent.at[2], NZ * (NX - 1) * REST)
+            landed(sent.at[3], NZ * NX * REST)
+
+        @pl.when((c == half) & (c == 0))
+        def _():
+            landed(sent.at[0], NX * SPLIT + (NZ - 1) * REST)
+
+        @pl.when((c == half) & (c == 1))
+        def _():
+            landed(sent.at[0], (NX - 1) * SPLIT + NZ * REST)
+
+        landed(sent.at[4], 8 * 128)
+        landed(sent.at[5], 128)
 
     my_block = span_ref[0, 0, me]
 
@@ -269,11 +305,11 @@
     def early(b, i):
         return span_ref[0, 0, index(b, i)] < my_block
 
-    def pick(buf, b):
+    def pick(at_row, b):
         e, both = [], []
         for i in range(NX):
-            blk = buf[b, i]
-            lo, hi = blk[:HALF], blk[HALF:]
+            lo = kv[b, i, at_row:at_row + HALF]
+            hi = kv[b, i, at_row + HALF:at_row + 2 * HALF]
             s = early(b, i)
             zero = jnp.zeros_like(lo)
             e.append(lo)
@@ -285,17 +321,17 @@
 
         @pl.when(c == 1)
         def _():
-            hand_over(vbuf, n).wait_recv()
+            hand_over(SECOND, n).wait_recv()
 
         @pl.when(c == 0)
         def _():
-            hand_over(kbuf, n).wait_recv()
-
-        ke, ksel = pick(kbuf, b)
+            hand_over(FIRST, n).wait_recv()
+
+        ke, ksel = pick(0, b)
         kselbuf[b] = ksel
         s1[b] = dot_nt(ke, qq[:, HD:]) * scale
         s2[b] = dot_nt(ksel, qq[...]) * scale
-        ve, vsel = pick(vbuf, b)
+        ve, vsel = pick(128, b)
         dp1[b] = dot_nt(ve, oo[:, HD:])
         dp2[b] = dot_nt(vsel, oo[...])
         old_e, old_l = state[0:1], state[1:2]
@@ -384,7 +420,7 @@
 
         @pl.when(i == LAG)
         def _():
-            landed(pqr.at[0], 8)
+            landed(pqr.at[0], 8 * 128)
             for kind in range(2):
                 for j in range(2):
                     lay_rows((qq, oo)[kind], ROWS, (pq, pg)[kind].at[j], 0, j)
@@ -405,7 +441,7 @@
         for i in range(3):
             sums_out[j, i:i + 1] = state[2 * i + j:2 * i + j + 1]
         swap_sums(j).start()
-    landed(sums_r.at[0])
+    landed(sums_r.at[0], 128)
     for j in range(2):
         m, l, d = (state[2 * i + j:2 * i + j + 1] for i in range(3))
         m2, l2, d2 = (
@@ -431,16 +467,16 @@
             diag[2 * j, :, :HD] = dot_nn(ds, qq[:, cols]) * INV_ROOT
             diag[2 * j, :, HD:2 * HD] = dot_nn(p.astype(BF16), oo[:, cols])
 
-    def give(buf, m):
-        b = row_of(NZ - 1 - m)
-        return remote(buf.at[b], sib.at[b], sent.at[6], sibr.at[m], sibling)
+    def give(part, m):
+        b = back_row(m)
+        return remote(pkv.at[b, :, part], sib.at[b, :, part], sent.at[6], sibr.at[m], sibling)
 
     def gradient_row(m):
-        b = row_of(NZ - 1 - m)
+        b = back_row(m)
         r_e, r_l, d_e, d_l = state[2:3], state[3:4], state[4:5], state[5:6]
         f_e = jnp.exp2(tops[b, 0:1] - state[0:1]) * r_e
         f_l = jnp.exp2(tops[b, 1:2] - state[1:2]) * r_l
-        ke = jnp.concatenate([kbuf[b, i, :HALF] for i in range(NX)], axis=0)
+        ke = jnp.concatenate([kv[b, i, :HALF] for i in range(NX)], axis=0)
         ksel = kselbuf[b]
         p1 = s1[b] * f_l
         ds1 = (p1 * (dp1[b] - d_l)).astype(BF16)
@@ -464,46 +500,48 @@
             part = slice(i * HALF, (i + 1) * HALF)
             s = early(b, i)
             zero = jnp.zeros((HALF, HD), F32)
-            cell = (b, i)
-            lo, hi = slice(0, HALF), slice(HALF, 2 * HALF)
-            pv[(*cell, lo)] = (v1[part] + jnp.where(s, v2[part, :HD], zero)).astype(BF16)
-            pv[(*cell, hi)] = jnp.where(s, zero, v2[part, HD:]).astype(BF16)
-            pk[(*cell, lo)] = (k1[part] + jnp.where(s, k2[part, :HD], zero)).astype(BF16)
-            pk[(*cell, hi)] = jnp.where(s, zero, k2[part, HD:]).astype(BF16)
+            k_lo, k_hi, v_lo, v_hi = (slice(j * HALF, (j + 1) * HALF) for j in range(4))
+            pkv[b, i, v_lo] = (v1[part] + jnp.where(s, v2[part, :HD], zero)).astype(BF16)
+            pkv[b, i, v_hi] = jnp.where(s, zero, v2[part, HD:]).astype(BF16)
+            pkv[b, i, k_lo] = (k1[part] + jnp.where(s, k2[part, :HD], zero)).astype(BF16)
+            pkv[b, i, k_hi] = jnp.where(s, zero, k2[part, HD:]).astype(BF16)
 
         @pl.when((m == NZ - 1) & (c == half))
         def _():
             for j in range(2):
                 part = slice(j * HALF, (j + 1) * HALF)
-                pk[z, x, part] = (pk[z, x, part].astype(F32) + diag[2 * j, :, :HD]).astype(BF16)
-                pv[z, x, part] = (pv[z, x, part].astype(F32) + diag[2 * j, :, HD:2 * HD]).astype(BF16)
+                v_part = slice(128 + j * HALF, 128 + (j + 1) * HALF)
+                pkv[z, x, part] = (
+                    pkv[z, x, part].astype(F32) + diag[2 * j, :, :HD]).astype(BF16)
+                pkv[z, x, v_part] = (
+                    pkv[z, x, v_part].astype(F32) + diag[2 * j, :, HD:2 * HD]).astype(BF16)
 
         @pl.when(c == 1)
         def _():
-            give(pv, m).start()
+            give(SECOND, m).start()
 
         @pl.when(c == 0)
         def _():
-            give(pk, m).start()
-
-    def add_into(dst, idx, *terms):
-        total = dst[idx].astype(F32)
+            give(FIRST, m).start()
+
+    def add_up(row, col, part, *terms):
+        total = pkv[row, col, part].astype(F32) + sib[row, col, part].astype(F32)
         for ref, i in terms:
             total = total + ref[i].astype(F32)
-        dst[idx] = total.astype(BF16)
+        return total
 
     def k_back(way, k, j):
         step = 1 if way == 0 else -1
         far = (1, 2, 1, 2)[k - 1]
-        return remote(pk.at[zoff(step * k), xoff(j)], rr.at[way, k - 1, j],
+        return remote(pkv.at[zoff(step * k), xoff(j), FIRST], rr.at[way, k - 1, j],
                       sent.at[7], rrsem.at[8 + j if k < 3 else way * 4 + j], at(zoff(step * far), x, 1))
 
     def k_across(j):
-        return remote(pk.at[z, xoff(j)], xr.at[j], sent.at[10], xrsem.at[0], at(z, xoff(j), 1))
+        return remote(pkv.at[z, xoff(j), FIRST], xr.at[j], sent.at[10], xrsem.at[0], at(z, xoff(j), 1))
 
     def k_hop(m):
-        give(pk, m).wait_recv()
-        d = ORDER[NZ - 1 - m]
+        give(FIRST, m).wait_recv()
+        d = BACK[m]
         k = abs(d)
         if k == 4:
             plan = [(w, j, ()) for i in range(2) for w, j in ((0, SETS[0][i]), (1, SETS[1][i]))]
@@ -516,82 +554,84 @@
             else:
                 plan = [(w, j, ()) for j in ACROSS]
         for w, j, has in plan:
-            cell = (zoff(d), xoff(j))
-            terms = [(sib, cell)]
+            row, col = zoff(d), xoff(j)
+            terms = []
             if has:
-                landed(rrsem.at[w * 4 + j], len(has))
+                landed(rrsem.at[w * 4 + j], len(has) * SPLIT)
             for q in has:
                 terms.append((rr, (w, q - 1, j)))
-            add_into(pk, cell, *terms)
+            pkv[row, col, FIRST] = add_up(row, col, FIRST, *terms).astype(BF16)
             k_back(w, k, j).start()
 
     def k_last():
-        give(pk, NZ - 1).wait_recv()
+        give(FIRST, NZ - 1).wait_recv()
         for j in (2, 1, 3, 0):
-            landed(rrsem.at[8 + j], 4)
-            cell = (z, xoff(j))
-            terms = [(sib, cell)]
+            landed(rrsem.at[8 + j], 4 * SPLIT)
+            terms = []
             for w in range(2):
                 for k in (1, 2):
                     terms.append((rr, (w, k - 1, j)))
-            add_into(pk, cell, *terms)
+            total = add_up(z, xoff(j), FIRST, *terms)
             if j:
+                pkv[z, xoff(j), FIRST] = total.astype(BF16)
                 k_across(j).start()
-        total = pk[z, x].astype(F32)
-        landed(xrsem.at[0], NX - 1)
+        landed(xrsem.at[0], (NX - 1) * SPLIT)
         for j in range(1, NX):
             total = total + xr[j].astype(F32)
-        ysum[...] = total.astype(BF16)
+        ysum[FIRST] = total.astype(BF16)
+
+    def cx_part(d, m):
+        return pl.ds((d * NZ + m) * REST, REST)
 
     def v_back(d, m):
-        return remote(pv.at[zoff(ORDER[NZ - 1 - m]), xoff(d)], cx.at[d * NZ + m], sent.at[8],
+        return remote(pkv.at[zoff(BACK[m]), xoff(d), SECOND], cx.at[cx_part(d, m)], sent.at[8],
                       c1r.at[m], at(z, xoff(d), 0))
 
     def v_z(m):
-        d = ORDER[NZ - 1 - m]
-        return remote(pv.at[zoff(d), x], zr.at[m], sent.at[9], zrsem.at[0], at(zoff(d), x, 0))
+        d = BACK[m]
+        return remote(pkv.at[zoff(d), x, SECOND], zr.at[m], sent.at[9], zrsem.at[0], at(zoff(d), x, 0))
 
     def v_out(m):
-        give(pv, m).wait_recv()
+        give(SECOND, m).wait_recv()
         for d in (2, 1, 3):
-            cell = (zoff(ORDER[NZ - 1 - m]), xoff(d))
-            add_into(pv, cell, (sib, cell))
+            row, col = zoff(BACK[m]), xoff(d)
+            pkv[row, col, SECOND] = add_up(row, col, SECOND).astype(BF16)
             v_back(d, m).start()
 
     def v_in(m):
-        cell = (zoff(ORDER[NZ - 1 - m]), x)
-        terms = [(sib, cell)]
-        landed(c1r.at[m], NX - 1)
-        for d in range(1, NX):
-            terms.append((cx, d * NZ + m))
-        add_into(pv, cell, *terms)
+        row = zoff(BACK[m])
+        landed(c1r.at[m], (NX - 1) * REST)
+        terms = [(cx, cx_part(d, m)) for d in range(1, NX)]
+        pkv[row, x, SECOND] = add_up(row, x, SECOND, *terms).astype(BF16)
         if m < NZ - 1:
             v_z(m).start()
 
     def v_last():
-        total = pv[z, x].astype(F32)
-        landed(zrsem.at[0], NZ - 1)
+        total = pkv[z, x, SECOND].astype(F32)
+        landed(zrsem.at[0], (NZ - 1) * REST)
         for m in range(NZ - 1):
             total = total + zr[m].astype(F32)
-        ysum[...] = total.astype(BF16)
+        ysum[SECOND] = total.astype(BF16)
 
     back = (
         {m: [(v_out, m - 2)] + ([(v_in, m - 6)] if m >= 6 else []) for m in range(2, NZ)},
-        {2: [(k_hop, 0)], 3: [(k_hop, 1)], 4: [(k_hop, 2)]},
+        {m: [(k_hop, m - 2)] for m in range(2, NZ - 1)},
     )
 
     def drain_scatter():
         @pl.when(c == 1)
         def _():
-            landed(sent.at[7], 28)
-            landed(sent.at[10], 3)
+            landed(sent.at[7], 28 * SPLIT)
+            landed(sent.at[10], (NX - 1) * SPLIT)
+            landed(sent.at[6], NZ * NX * REST)
+            landed(sent.at[11], NT * SPLIT)
 
         @pl.when(c == 0)
         def _():
-            landed(sent.at[8], 24)
-            landed(sent.at[9], 7)
-
-        landed(sent.at[6], 32)
+            landed(sent.at[8], NZ * (NX - 1) * REST)
+            landed(sent.at[9], (NZ - 1) * REST)
+            landed(sent.at[6], NZ * NX * SPLIT)
+            landed(sent.at[11], NT * REST)
 
     def scatter_step(m, _):
         gradient_row(m)
@@ -609,8 +649,8 @@
 
     @pl.when(c == 1)
     def _():
-        for m in range(3, NZ - 1):
-            k_hop(m)
+        k_hop(5)
+        k_hop(6)
 
     for j, acc in enumerate((dq2[0:HD], dq2[HD:2 * HD] + dql[...])):
         g = (acc * INV_ROOT).T.astype(BF16)
@@ -639,23 +679,26 @@
             v_in(m)
         v_last()
 
-    def last(tt):
-        return remote(ysum, yr.at[1 - c, t // 2], sent.at[11], yrsem.at[0],
+    def last(tt, part):
+        return remote(ysum.at[part], yr.at[t // 2, part], sent.at[11], yrsem.at[0],
                       other(tt, half))
 
-    for tt in range(NT):
-        last(tt).start()
+    for core, part in ((0, SECOND), (1, FIRST)):
+        @pl.when(c == core)
+        def _():
+            for tt in range(NT):
+                last(tt, part).start()
 
     drain_gather()
     drain_scatter()
 
-    landed(dqsr.at[0], 8)
+    landed(dqsr.at[0], 8 * 128)
     dq_out[0] = (dqr[0].astype(F32) + dqr[1].astype(F32)).astype(BF16)
-    landed(yrsem.at[0], 4)
+    landed(yrsem.at[0], 2 * BLOCK)
     for kind, out in ((0, dk_out), (1, dv_out)):
-        out[0] = (yr[kind, 0].astype(F32) + yr[kind, 1].astype(F32)).astype(BF16)
-    landed(sent.at[11], 4)
-    landed(sent.at[12], 8)
+        part = slice(kind * 128, (kind + 1) * 128)
+        out[0] = (yr[0, part].astype(F32) + yr[1, part].astype(F32)).astype(BF16)
+    landed(sent.at[12], 8 * 128)
 
 
 def per_device(queries, keys, values, grad_out, span_order):
@@ -664,14 +707,13 @@
     dma = pltpu.SemaphoreType.DMA
 
     def plane():
-        return pltpu.VMEM((NZ, NX, 128, HD), BF16)
+        return pltpu.VMEM((NZ, NX, BLOCK, HD), BF16)
 
     scratch = [
         pltpu.VMEM(queries.shape, BF16),
         pltpu.VMEM(keys.shape, BF16),
         pltpu.VMEM(values.shape, BF16),
         pltpu.VMEM(grad_out.shape, BF16),
-        plane(),
         plane(),
         pltpu.VMEM((NZ, KEYS, SLOTS), F32),
         pltpu.VMEM((NZ, KEYS, SLOTS), F32),
@@ -693,13 +735,12 @@
         pltpu.VMEM((2, 8, SLOTS), F32),
         plane(),
         plane(),
-        plane(),
-        pltpu.VMEM((2, 4, NX, 128, HD), BF16),
-        pltpu.VMEM((NX * NZ, 128, HD), BF16),
-        pltpu.VMEM((NZ, 128, HD), BF16),
-        pltpu.VMEM((NX, 128, HD), BF16),
-        pltpu.VMEM((128, HD), BF16),
-        pltpu.VMEM((2, 2, 128, HD), BF16),
+        pltpu.VMEM((2, 4, NX, SPLIT, HD), BF16),
+        pltpu.VMEM((NX * NZ * REST, HD), BF16),
+        pltpu.VMEM((NZ, REST, HD), BF16),
+        pltpu.VMEM((NX, SPLIT, HD), BF16),
+        pltpu.VMEM((BLOCK, HD), BF16),
+        pltpu.VMEM((2, BLOCK, HD), BF16),
         dma((2,)), dma((13,)),
         dma((NX,)), dma((NZ,)), dma((13,)), dma((NZ,)), dma((NZ,)),
         dma((1,)), dma((1,)),

time: 65.2 us -> 63.2 us (0.969)
  Pallas kernels: 61.3 us -> 59.3 us
    pallas_call x1, Pallas kernels: 61.3 us -> 59.3 us  [per_device(): pl.pallas_call(kernel, out_shape=(jax.ShapeDtypeStruct(queries.shape, BF1...]
where the time goes in v5:
time: 63.2 us; the launch traced here: 62.9 us
  Pallas kernels  59.3 us (94%)
  local copies, waits for them, and re-layouts  2.96 us (5%)
  between operations  0.65 us (1%)
    pallas_call x1, Pallas kernels, per_device(): pl.pallas_call(kernel, out_shape=(jax.ShapeDtypeStruct(queries.shape, BF1...  59.3 us
    unnamed x7, local copies, waits for them, and re-layouts  2.96 us

profile of v5, /device:TPU:1, one launch (start us, length us, event | category | flops | bytes accessed | tf_op | source)
XLA Modules:
  0.0 62.9 jit_solution(3204896726433451626)
XLA Ops:
  0.6 59.3 %attention_backward.1 = (bf16[1,128,512]{2,1,0:T(8,128)(2,1)}, bf16[1,128,128]{2,1,0:T(8,128)(2,1)}, bf16[1,128,128]{2,1,0:T(8,128)(2,1)}) custom-call(bf16[1,128,512]{2,1,0:T(8,128)(2,1)} %q_hbm.1, bf16[1,128,128]{2,1,0:T(8,128)(2,1)} %k_hbm.1, bf16[1,128,128]{2,1,0:T(8,128)(2,1)} %v_hbm.1, bf16[1,128,512]{2,1,0:T(8,128)(2,1)} %g_hbm.1, s32[1,2,64]{2,1,0:T(2,128)} %bitcast.1), custom_call_target="tpu_custom_call" | custom-call | tf_op jit(solution)/shard_map/attention_backward/pallas_call | solution.py:750
  60.0 0.0 copy-start.1
  60.0 1.6 %copy.11 = bf16[1,128,512]{2,1,0:T(8,128)(2,1)} copy(bf16[1,128,512]{2,1,0:T(8,128)(2,1)} %get-tuple-element.6) | data formatting | bytes 262144
  61.5 0.0 copy-done.1
  61.5 0.0 copy-start
  61.5 0.6 copy.12
  62.2 0.2 copy-done
  62.3 0.6 copy.13
Async XLA Ops:
  60.0 1.6 %copy-start.1 = (bf16[1,128,128]{2,1,0:T(8,128)(2,1)S(1)}, bf16[1,128,128]{2,1,0:T(8,128)(2,1)}, u32[]{:S(2)}) copy-start(bf16[1,128,128]{2,1,0:T(8,128)(2,1)} %get-tuple-element.7) | copy-start | bytes 98308
  61.5 0.8 %copy-start = (bf16[1,128,128]{2,1,0:T(8,128)(2,1)S(1)}, bf16[1,128,128]{2,1,0:T(8,128)(2,1)}, u32[]{:S(2)}) copy-start(bf16[1,128,128]{2,1,0:T(8,128)(2,1)} %get-tuple-element.8) | copy-start | bytes 98308

commit v6 on v5

--- a/solution.py
+++ b/solution.py
@@ -57,10 +57,10 @@
 
 def kernel(
     q_hbm, k_hbm, v_hbm, g_hbm, span_ref,
-    dq_out, dk_out, dv_out,
-    q_ref, k_ref, v_ref, g_ref, kv, s1, s2, dp1, dp2, kselbuf, qq, oo, pq, pg, dql, dq2, dqst, dqr,
+    dqr, yr,
+    q_ref, k_ref, v_ref, g_ref, kv, s1, s2, dp1, dp2, kselbuf, qq, oo, pq, pg, dql, dq2, dqst,
     state, tops, diag, sums_out, sums_in,
-    pkv, sib, rr, cx, zr, xr, ysum, yr,
+    pkv, sib, rr, cx, zr, xr, ysum,
     insem, sent, p1kr, p1vr, zkr, x1r, d2dr, pqr, sums_r, sibr, rrsem, c1r, zrsem, xrsem,
     yrsem, dqsr,
 ):
@@ -693,12 +693,15 @@
     drain_scatter()
 
     landed(dqsr.at[0], 8 * 128)
+    landed(yrsem.at[0], 2 * BLOCK)
+    landed(sent.at[12], 8 * 128)
+
+
+def last_sums(dqr, yr, dq_out, dk_out, dv_out):
     dq_out[0] = (dqr[0].astype(F32) + dqr[1].astype(F32)).astype(BF16)
-    landed(yrsem.at[0], 2 * BLOCK)
     for kind, out in ((0, dk_out), (1, dv_out)):
         part = slice(kind * 128, (kind + 1) * 128)
         out[0] = (yr[0, part].astype(F32) + yr[1, part].astype(F32)).astype(BF16)
-    landed(sent.at[12], 8 * 128)
 
 
 def per_device(queries, keys, values, grad_out, span_order):
@@ -727,7 +730,6 @@
         pltpu.VMEM((HD, SLOTS), F32),
         pltpu.VMEM((2 * HD, SLOTS), F32),
         pltpu.VMEM((2, 128, HEADS * HD), BF16),
-        pltpu.VMEM((2, 128, HEADS * HD), BF16),
         pltpu.VMEM((8, SLOTS), F32),
         pltpu.VMEM((NZ + 1, 8, SLOTS), F32),
         pltpu.VMEM((4, HALF, SLOTS), F32),
@@ -740,28 +742,33 @@
         pltpu.VMEM((NZ, REST, HD), BF16),
         pltpu.VMEM((NX, SPLIT, HD), BF16),
         pltpu.VMEM((BLOCK, HD), BF16),
-        pltpu.VMEM((2, BLOCK, HD), BF16),
         dma((2,)), dma((13,)),
         dma((NX,)), dma((NZ,)), dma((13,)), dma((NZ,)), dma((NZ,)),
         dma((1,)), dma((1,)),
         dma((NZ,)), dma((12,)), dma((NZ,)), dma((1,)), dma((1,)),
         dma((1,)), dma((1,)),
     ]
-    return pl.pallas_call(
+    arrived = pl.pallas_call(
         kernel,
         out_shape=(
-            jax.ShapeDtypeStruct(queries.shape, BF16),
-            jax.ShapeDtypeStruct(keys.shape, BF16),
-            jax.ShapeDtypeStruct(values.shape, BF16),
+            jax.ShapeDtypeStruct((2, 128, HEADS * HD), BF16),
+            jax.ShapeDtypeStruct((2, BLOCK, HD), BF16),
         ),
         in_specs=[hbm, hbm, hbm, hbm, pl.BlockSpec(memory_space=pltpu.SMEM)],
-        out_specs=(vmem, vmem, vmem),
+        out_specs=(hbm, hbm),
         scratch_shapes=scratch,
         compiler_params=pltpu.CompilerParams(
             collective_id=1, has_side_effects=True, vmem_limit_bytes=56 * 2**20
         ),
         name="attention_backward",
     )(queries, keys, values, grad_out, jnp.swapaxes(span_order, 1, 2))
+    return pl.pallas_call(
+        last_sums,
+        out_shape=tuple(jax.ShapeDtypeStruct(a.shape, BF16) for a in (queries, keys, values)),
+        in_specs=[vmem, vmem],
+        out_specs=(vmem, vmem, vmem),
+        name="last_sums",
+    )(*arrived)
 
 
 def solution(mesh):

time: 63.2 us -> 61.3 us (0.970)
  local copies, waits for them, and re-layouts: 2.96 us -> 0 us
  Pallas kernels: 59.3 us -> 60.5 us
    unnamed x7 -> x0, local copies, waits for them, and re-layouts: 2.96 us -> none
    pallas_call x1 -> x2, Pallas kernels: 59.3 us -> 60.5 us  [the longest x1 58.8 us: per_device(): pl.pallas_call(kernel, out_shape=(jax.ShapeDtypeStruct((2, 128, HEADS * H...]
where the time goes in v6:
time: 61.3 us; the launch traced here: 61.1 us
  Pallas kernels  60.5 us (99%)
  between operations  0.64 us (1%)
    pallas_call x1, Pallas kernels, per_device(): pl.pallas_call(kernel, out_shape=(jax.ShapeDtypeStruct((2, 128, HEADS * H...  58.8 us
    pallas_call x1, Pallas kernels, per_device(): pl.pallas_call(last_sums, out_shape=tuple((jax.ShapeDtypeStruct(a.shape,...  1.68 us

profile of v6, /device:TPU:1, one launch (start us, length us, event | category | flops | bytes accessed | tf_op | source)
XLA Modules:
  0.0 61.1 jit_solution(16296631723120495511)
XLA Ops:
  0.6 58.8 %attention_backward.1 = (bf16[2,128,512]{2,1,0:T(8,128)(2,1)}, bf16[2,256,128]{2,1,0:T(8,128)(2,1)}) custom-call(bf16[1,128,512]{2,1,0:T(8,128)(2,1)} %q_hbm.1, bf16[1,128,128]{2,1,0:T(8,128)(2,1)} %k_hbm.1, bf16[1,128,128]{2,1,0:T(8,128)(2,1)} %v_hbm.1, bf16[1,128,512]{2,1,0:T(8,128)(2,1)} %g_hbm.1, s32[1,2,64]{2,1,0:T(2,128)} %bitcast.1), custom_call_target="tpu_custom_call" | custom-call | tf_op jit(solution)/shard_map/attention_backward/pallas_call | solution.py:751
  59.4 1.7 %last_sums.1 = (bf16[1,128,512]{2,1,0:T(8,128)(2,1)}, bf16[1,128,128]{2,1,0:T(8,128)(2,1)}, bf16[1,128,128]{2,1,0:T(8,128)(2,1)}) custom-call(bf16[2,128,512]{2,1,0:T(8,128)(2,1)} %get-tuple-element.5.dqr, bf16[2,256,128]{2,1,0:T(8,128)(2,1)} %get-tuple-element.6.yr), custom_call_target="tpu_custom_call" | custom-call | tf_op jit(solution)/shard_map/last_sums/pallas_call | solution.py:765

commit v7 on v6

--- a/solution.py
+++ b/solution.py
@@ -403,7 +403,7 @@
         {
             0: [(gather_k, 0), (gather_k, 3), (gather_k, 4)],
             1: [(gather_k, 1), (gather_k, 2)],
-            6: [(gather_k, 5), (gather_k, 6), (gather_k, 7)],
+            5: [(gather_k, 5), (gather_k, 6), (gather_k, 7)],
         },
     )
 

time: 61.3 us -> 61.6 us (level)
  no operation moved by 1% of the time
where the time goes in v7:
time: 61.6 us; the launch traced here: 61.3 us
  Pallas kernels  60.7 us (99%)
  between operations  0.64 us (1%)
    pallas_call x1, Pallas kernels, per_device(): pl.pallas_call(kernel, out_shape=(jax.ShapeDtypeStruct((2, 128, HEADS * H...  59 us
    pallas_call x1, Pallas kernels, per_device(): pl.pallas_call(last_sums, out_shape=tuple((jax.ShapeDtypeStruct(a.shape,...  1.68 us

profile of v7, /device:TPU:1, one launch (start us, length us, event | category | flops | bytes accessed | tf_op | source)
XLA Modules:
  0.0 61.3 jit_solution(6522649177854448269)
XLA Ops:
  0.6 59.0 %attention_backward.1 = (bf16[2,128,512]{2,1,0:T(8,128)(2,1)}, bf16[2,256,128]{2,1,0:T(8,128)(2,1)}) custom-call(bf16[1,128,512]{2,1,0:T(8,128)(2,1)} %q_hbm.1, bf16[1,128,128]{2,1,0:T(8,128)(2,1)} %k_hbm.1, bf16[1,128,128]{2,1,0:T(8,128)(2,1)} %v_hbm.1, bf16[1,128,512]{2,1,0:T(8,128)(2,1)} %g_hbm.1, s32[1,2,64]{2,1,0:T(2,128)} %bitcast.1), custom_call_target="tpu_custom_call" | custom-call | tf_op jit(solution)/shard_map/attention_backward/pallas_call | solution.py:751
  59.7 1.7 %last_sums.1 = (bf16[1,128,512]{2,1,0:T(8,128)(2,1)}, bf16[1,128,128]{2,1,0:T(8,128)(2,1)}, bf16[1,128,128]{2,1,0:T(8,128)(2,1)}) custom-call(bf16[2,128,512]{2,1,0:T(8,128)(2,1)} %get-tuple-element.5.dqr, bf16[2,256,128]{2,1,0:T(8,128)(2,1)} %get-tuple-element.6.yr), custom_call_target="tpu_custom_call" | custom-call | tf_op jit(solution)/shard_map/last_sums/pallas_call | solution.py:765

commit v8 on v6

--- a/solution.py
+++ b/solution.py
@@ -154,10 +154,6 @@
         src = (q_hbm, g_hbm)[kind].at[0, pl.ds(j * HALF, HALF)]
         dst = (pq, pg)[kind].at[j]
         return remote(src, dst, sent.at[4], pqr.at[0], mate(j))
-
-    for kind in range(2):
-        for j in range(2):
-            swap_rows(j, kind).start()
 
     def first_k(d):
         return remote(k_hbm.at[0, FIRST], kv.at[z, x, FIRST], sent.at[0], p1kr.at[d],
@@ -262,6 +258,12 @@
             for cp in first_v(d):
                 cp.start()
 
+    for kind in range(2):
+        for j in range(2):
+            swap_rows(j, kind).start()
+
+    @pl.when(c == half)
+    def _():
         @pl.when(c == 0)
         def _():
             landed(insem.at[1], REST)

time: 61.3 us -> 61.4 us (level)
  no operation moved by 1% of the time
where the time goes in v8:
time: 61.4 us; the launch traced here: 61.1 us
  Pallas kernels  60.5 us (99%)
  between operations  0.64 us (1%)
    pallas_call x1, Pallas kernels, per_device(): pl.pallas_call(kernel, out_shape=(jax.ShapeDtypeStruct((2, 128, HEADS * H...  58.8 us
    pallas_call x1, Pallas kernels, per_device(): pl.pallas_call(last_sums, out_shape=tuple((jax.ShapeDtypeStruct(a.shape,...  1.68 us

profile of v8, /device:TPU:1, one launch (start us, length us, event | category | flops | bytes accessed | tf_op | source)
XLA Modules:
  0.0 61.1 jit_solution(1860307083371957983)
XLA Ops:
  0.6 58.8 %attention_backward.1 = (bf16[2,128,512]{2,1,0:T(8,128)(2,1)}, bf16[2,256,128]{2,1,0:T(8,128)(2,1)}) custom-call(bf16[1,128,512]{2,1,0:T(8,128)(2,1)} %q_hbm.1, bf16[1,128,128]{2,1,0:T(8,128)(2,1)} %k_hbm.1, bf16[1,128,128]{2,1,0:T(8,128)(2,1)} %v_hbm.1, bf16[1,128,512]{2,1,0:T(8,128)(2,1)} %g_hbm.1, s32[1,2,64]{2,1,0:T(2,128)} %bitcast.1), custom_call_target="tpu_custom_call" | custom-call | tf_op jit(solution)/shard_map/attention_backward/pallas_call | solution.py:753
  59.5 1.7 %last_sums.1 = (bf16[1,128,512]{2,1,0:T(8,128)(2,1)}, bf16[1,128,128]{2,1,0:T(8,128)(2,1)}, bf16[1,128,128]{2,1,0:T(8,128)(2,1)}) custom-call(bf16[2,128,512]{2,1,0:T(8,128)(2,1)} %get-tuple-element.5.dqr, bf16[2,256,128]{2,1,0:T(8,128)(2,1)} %get-tuple-element.6.yr), custom_call_target="tpu_custom_call" | custom-call | tf_op jit(solution)/shard_map/last_sums/pallas_call | solution.py:767
